TPU v7x, 128 devices: a whole 4x4x4 slice. The times are simulated.
128 devices in a mesh: group: 4 (over y), local: 32 (over z, x, core).
Axes of the slice: x: 4, y: 4, z: 4, core: 2. Of those that a mesh axis runs over, the one named last changes fastest.
Arguments:
- tokens: bfloat16 [8192, 7168], P(('group', 'local')), may hold values from -6 to 6
- routes: int32 [8192, 8], P(('group', 'local')), may hold values from 0 to 63, all different within a row; in each aligned block of 64 rows (0 to 63, 64 to 127, ...) at most 10 rows name the same one
- gates: float32 [8192, 8], P(('group', 'local')), may hold values from 0.05 to 1
- gate_weight: bfloat16 [128, 7168, 512], P(('group', 'local')), may hold values from -0.0625 to 0.0625
- up_weight: bfloat16 [128, 7168, 512], P(('group', 'local')), may hold values from -0.0625 to 0.0625
- down_weight: bfloat16 [128, 512, 7168], P(('group', 'local')), may hold values from -0.1875 to 0.1875
Outputs:
- mixed: bfloat16 [8192, 7168], P(('group', 'local'))
Inputs may be any that keep to these rules, and one draw needn't show every extreme that they name: `routes`: each row names 8 different experts. Among the 64 rows of one device no expert is named by more than 10 rows, a bound that some block reaches.
All inputs are finite; a program needn't handle non-finite values.
Results may differ from a plain program's by a relative error of at most 0.0065.
Values may be sent and summed in bfloat16 or wider, within the bound.
No kernel may reach another device: no remote copies, remote signals or barrier semaphores. Data moves between devices by JAX's collectives and lax.ppermute only.
A program may use at most 192 MiB of HBM per device.

v0:
```python
import jax
import jax.numpy as jnp
from jax import lax
from jax.sharding import PartitionSpec as P


def from_partner(x, axis, stride):
    return lax.ppermute(x, axis, [(i, i ^ 1 << stride) for i in range(lax.axis_size(axis))])


def send_rows(outgoing):
    return lax.all_to_all(outgoing, ("group", "local"), split_axis=0, concat_axis=0, tiled=True)


def return_rows(finished):
    return lax.all_to_all(finished, ("group", "local"), split_axis=0, concat_axis=0, tiled=True)


def slot_ranks(route_rows, experts):
    hits = (route_rows[..., None] == jnp.arange(experts, dtype=jnp.int32)).astype(jnp.int32)
    earlier = jnp.cumsum(hits, axis=-2) - hits
    return jnp.sum(earlier * hits, axis=-1)


def local(tokens, routes, gates, gate_weight, up_weight, down_weight):
    tok_rows, width = tokens.shape
    chosen = routes.shape[1]
    groups = lax.axis_size("group")
    members = lax.axis_size("local")
    devices = groups * members
    experts = devices // 2
    capacity = 5 * tok_rows * chosen // (4 * experts)
    halfcap = capacity // 2
    share = lax.axis_index("local") % 2
    flat_routes = routes.reshape(-1)
    ranking = slot_ranks(flat_routes, experts)
    places = flat_routes * capacity + ranking
    picks_flat = places[:, None] == jnp.arange(experts * capacity, dtype=jnp.int32)[None, :]
    picks_flat = picks_flat.astype(jnp.bfloat16).reshape(tok_rows, chosen, experts * capacity)
    packer = jnp.sum(picks_flat, axis=1)
    packed = jnp.einsum("tc,td->cd", packer, tokens, preferred_element_type=jnp.float32).astype(
        jnp.bfloat16
    )
    raw = send_rows(packed.reshape(devices, halfcap, width))
    theirs = from_partner(raw, "local", 0)
    leading = jnp.where(share == 0, raw, theirs)
    trailing = jnp.where(share == 0, theirs, raw)
    arrived = jnp.concatenate([leading, trailing], axis=1)
    rows_in = arrived.reshape(-1, width)
    gate_val = jnp.dot(rows_in, gate_weight[0], preferred_element_type=jnp.float32)
    up_val = jnp.dot(rows_in, up_weight[0], preferred_element_type=jnp.float32)
    hidden = (jax.nn.silu(gate_val) * up_val).astype(jnp.bfloat16)
    partial_out = jnp.dot(hidden, down_weight[0], preferred_element_type=jnp.float32).astype(
        jnp.bfloat16
    )
    partial_out = partial_out.reshape(devices, capacity, width)
    kept = lax.dynamic_slice_in_dim(partial_out, share * halfcap, halfcap, 1)
    given = lax.dynamic_slice_in_dim(partial_out, (1 - share) * halfcap, halfcap, 1)
    partner = from_partner(given, "local", 0)
    kept_wide = lax.optimization_barrier(kept).astype(jnp.float32)
    summed = (kept_wide + partner.astype(jnp.float32)).astype(jnp.bfloat16)
    returned = return_rows(summed)
    returned = returned.reshape(experts * capacity, width)
    picked = returned[places].reshape(tok_rows, chosen, width)
    mixed = jnp.sum(picked.astype(jnp.float32) * gates[:, :, None], axis=1)
    return mixed.astype(jnp.bfloat16)


def solution(mesh):
    placed = (
        P(("group", "local"), None),
        P(("group", "local"), None),
        P(("group", "local"), None),
        P(("group", "local"), None, None),
        P(("group", "local"), None, None),
        P(("group", "local"), None, None),
    )
    return jax.shard_map(
        local, mesh=mesh, in_specs=placed, out_specs=P(("group", "local"), None), check_vma=False
    )
```

profile of v0, /device:TPU:12, one launch (start us, length us, event | category | flops | bytes accessed | tf_op | source)
XLA Modules:
  0.0 685.6 jit_solution(10595096023874401466)
XLA Ops:
  0.0 0.9 copy.24
  0.9 0.1 eq.50
  0.9 0.1 eq.46
  1.1 1.2 reduce-window.6
  2.3 0.2 slice_reduce_fusion
  2.5 0.1 fusion.11
  2.8 0.6 broadcast_multiply_fusion
  3.4 0.5 fusion.8
  3.9 6.1 convolution_convert_fusion.1
  10.0 14.8 %reshape.77 = bf16[128,5,7168]{2,1,0:T(8,128)(2,1)} reshape(bf16[640,7168]{1,0:T(8,128)(2,1)} %convolution_convert_fusion.1) | data formatting | bytes 18350080 | tf_op jit(solution)/shard_map/reshape | solution.py:44
  24.7 175.1 %all_to_all.10 = bf16[128,5,7168]{2,1,0:T(8,128)(2,1)S(1)} all-to-all(bf16[128,5,7168]{2,1,0:T(8,128)(2,1)} %reshape.77), channel_id=1, replica_groups=mesh['group'=4,'local'=32] {'group','local'}, dimensions={0} | all-to-all | bytes 18350080 | tf_op jit(solution)/shard_map/all_to_all | solution.py:12
  199.8 8.3 %copy.28 = bf16[128,5,7168]{2,0,1:T(8,128)(2,1)} copy(bf16[128,5,7168]{2,1,0:T(8,128)(2,1)S(1)} %all_to_all.10) | data formatting | bytes 18350080 | tf_op jit(solution)/shard_map/all_to_all | solution.py:12
  208.1 0.4 collective-permute-start
  208.5 14.5 %collective-permute-done = bf16[128,5,7168]{2,0,1:T(8,128)(2,1)} collective-permute-done((bf16[128,5,7168]{2,0,1:T(8,128)(2,1)}, bf16[128,5,7168]{2,0,1:T(8,128)(2,1)}, u32[]{:S(2)}, u32[]{:S(2)}) %collective-permute-start) | collective-permute-done | bytes 9175072 | tf_op jit(solution)/shard_map/ppermute | solution.py:8
  223.0 22.3 %copy_select_fusion.1 = (bf16[128,5,7168]{2,1,0:T(8,128)(2,1)}, bf16[128,5,7168]{2,1,0:T(8,128)(2,1)}) fusion(bf16[128,5,7168]{2,1,0:T(8,128)(2,1)} %copy-done.2, bf16[128,5,7168]{2,0,1:T(8,128)(2,1)} %collective-permute-done, pred[]{:T(512)S(6)} %eq.45), kind=kLoop, calls=%fused_computation.5 | loop fusion | flops 9175040 | bytes 36700160 | tf_op jit(solution)/shard_map/jit(_where)/select_n | solution.py:46
  245.4 20.5 %pad_maximum_fusion = bf16[128,10,7168]{2,1,0:T(8,128)(2,1)} fusion(bf16[128,5,7168]{2,1,0:T(8,128)(2,1)} %get-tuple-element.8, bf16[128,5,7168]{2,1,0:T(8,128)(2,1)} %get-tuple-element.7), kind=kLoop, calls=%fused_computation.1 | loop fusion | flops 36700160 | bytes 36700160 | tf_op jit(solution)/shard_map/concatenate | solution.py:48
  265.9 28.3 %reshape.78 = bf16[1280,7168]{1,0:T(8,128)(2,1)} reshape(bf16[128,10,7168]{2,1,0:T(8,128)(2,1)} %pad_maximum_fusion) | data formatting | bytes 36700160 | tf_op jit(solution)/shard_map/reshape | solution.py:49
  294.1 15.3 %fusion.2 = f32[1280,512]{1,0:T(8,128)S(1)} fusion(bf16[1280,7168]{1,0:T(8,128)(2,1)} %reshape.78, bf16[1,7168,512]{2,1,0:T(8,128)(2,1)} %param.10), kind=kOutput, calls=%fused_computation.10 | convolution fusion | flops 9395240960 | bytes 28311552 | tf_op jit(solution)/shard_map/dot_general | solution.py:51
  309.4 13.6 %fusion.4 = f32[1280,512]{1,0:T(8,128)} fusion(bf16[1280,7168]{1,0:T(8,128)(2,1)S(1)} %copy-done.3, bf16[1,7168,512]{2,1,0:T(8,128)(2,1)} %param.9), kind=kOutput, calls=%fused_computation.12 | convolution fusion | flops 9395240960 | bytes 28311552 | tf_op jit(solution)/shard_map/dot_general | solution.py:50
  323.0 16.6 %convolution_convert_fusion = bf16[1280,7168]{1,0:T(8,128)(2,1)} fusion(bf16[1,512,7168]{2,1,0:T(8,128)(2,1)} %param.11, f32[1280,512]{1,0:T(8,128)S(1)} %fusion.2, f32[1280,512]{1,0:T(8,128)} %fusion.4), kind=kOutput, calls=%fused_computation.3 | convolution fusion | flops 9408348160 | bytes 30932992 | tf_op jit(solution)/shard_map/dot_general | solution.py:53
  339.5 28.2 %reshape.79 = bf16[128,10,7168]{2,1,0:T(8,128)(2,1)} reshape(bf16[1280,7168]{1,0:T(8,128)(2,1)} %convolution_convert_fusion) | data formatting | bytes 36700160 | tf_op jit(solution)/shard_map/reshape | solution.py:56
  367.8 28.6 %constant_dynamic-slice_fusion = (bf16[128,5,7168]{2,1,0:T(8,128)(2,1)}, bf16[128,5,7168]{2,1,0:T(8,128)(2,1)S(1)}) fusion(bf16[128,10,7168]{2,1,0:T(8,128)(2,1)} %reshape.79, s32[]{:T(128)S(6)} %select_n.40, s32[]{:T(128)S(6)} %select_n.39), kind=kLoop, calls=%fused_computation.31 | loop fusion | bytes 36700168 | tf_op jit(solution)/shard_map/dynamic_slice | solution.py:58
  396.4 10.6 %copy.31 = bf16[128,5,7168]{2,0,1:T(8,128)(2,1)S(1)} copy(bf16[128,5,7168]{2,1,0:T(8,128)(2,1)} %get-tuple-element.5) | data formatting | bytes 18350080 | tf_op jit(solution)/shard_map/dynamic_slice | solution.py:58
  407.0 0.2 collective-permute-start.1
  407.2 14.1 %collective-permute-done.1 = bf16[128,5,7168]{2,0,1:T(8,128)(2,1)S(1)} collective-permute-done((bf16[128,5,7168]{2,0,1:T(8,128)(2,1)S(1)}, bf16[128,5,7168]{2,0,1:T(8,128)(2,1)S(1)}, u32[]{:S(2)}, u32[]{:S(2)}) %collective-permute-start.1) | collective-permute-done | bytes 9175072 | tf_op jit(solution)/shard_map/ppermute | solution.py:8
  421.4 11.0 %add_convert_fusion = bf16[128,5,7168]{2,1,0:T(8,128)(2,1)} fusion(bf16[128,5,7168]{2,1,0:T(8,128)(2,1)S(1)} %get-tuple-element.6, bf16[128,5,7168]{2,0,1:T(8,128)(2,1)S(1)} %collective-permute-done.1), kind=kLoop, calls=%fused_computation.2 | loop fusion | flops 18350080 | bytes 27525120 | tf_op jit(solution)/shard_map/convert_element_type | solution.py:61
  432.4 9.4 %all-to-all-start.1 = ((bf16[128,5,7168]{2,1,0:T(8,128)(2,1)}), bf16[128,5,7168]{2,1,0:T(8,128)(2,1)}, u32[]{:S(2)}, u32[]{:S(2)}) async-start(bf16[128,5,7168]{2,1,0:T(8,128)(2,1)} %add_convert_fusion), calls=%async_computation.1 | async-start | bytes 29360128 | tf_op jit(solution)/shard_map/all_to_all | solution.py:16
  441.9 0.1 mul.50
  442.1 199.5 %all-to-all-done.1 = bf16[128,5,7168]{2,1,0:T(8,128)(2,1)} async-done(((bf16[128,5,7168]{2,1,0:T(8,128)(2,1)}), bf16[128,5,7168]{2,1,0:T(8,128)(2,1)}, u32[]{:S(2)}, u32[]{:S(2)}) %all-to-all-start.1) | async-done | bytes 9175072 | tf_op jit(solution)/shard_map/all_to_all | solution.py:16
  641.6 15.1 %reshape.80 = bf16[640,7168]{1,0:T(8,128)(2,1)} reshape(bf16[128,5,7168]{2,1,0:T(8,128)(2,1)} %all-to-all-done.1) | data formatting | bytes 18350080 | tf_op jit(solution)/shard_map/reshape | solution.py:63
  656.7 18.9 %gather_fusion = bf16[512,7168]{1,0:T(8,128)(2,1)} fusion(bf16[640,7168]{1,0:T(8,128)(2,1)} %reshape.80, s32[1024]{0:T(1024)S(1)} %pad_clamp_fusion), kind=kCustom, calls=%fused_computation | custom fusion | bytes 14682112 | tf_op jit(solution)/shard_map/gather | solution.py:64
  675.5 9.8 %fusion = bf16[64,7168]{1,0:T(8,128)(2,1)} fusion(bf16[512,7168]{1,0:T(8,128)(2,1)} %gather_fusion, f32[64,8]{1,0:T(8,128)S(1)} %copy.33), kind=kLoop, calls=%fused_computation.7 | loop fusion | flops 10551296 | bytes 8259584 | tf_op jit(solution)/shard_map/reduce_sum | solution.py:65
  (23 shorter events, 0.3 us)
Async XLA Ops:
  0.0 3.8 copy-start
  2.7 22.1 %copy-start.5 = (s32[512]{0:T(512)}, s32[512]{0:T(512)S(1)}, u32[]{:S(2)}) copy-start(s32[512]{0:T(512)S(1)} %fusion.11) | copy-start | bytes 6148
  199.8 8.3 %copy-start.2 = (bf16[128,5,7168]{2,1,0:T(8,128)(2,1)}, bf16[128,5,7168]{2,1,0:T(8,128)(2,1)S(1)}, u32[]{:S(2)}) copy-start(bf16[128,5,7168]{2,1,0:T(8,128)(2,1)S(1)} %all_to_all.10) | copy-start | bytes 27525124
  208.1 14.9 %collective-permute-start = (bf16[128,5,7168]{2,0,1:T(8,128)(2,1)}, bf16[128,5,7168]{2,0,1:T(8,128)(2,1)}, u32[]{:S(2)}, u32[]{:S(2)}) collective-permute-start(bf16[128,5,7168]{2,0,1:T(8,128)(2,1)} %copy.28), channel_id=1, source_target_pairs={{0,1},{1,0},{2,3},{3,2},{4,5},{5,4},{6,7},{7,6},{8,9},{9,8},{10,11... | collective-permute-start | bytes 27525128 | tf_op jit(solution)/shard_map/ppermute | solution.py:8
  294.1 15.3 %copy-start.3 = (bf16[1280,7168]{1,0:T(8,128)(2,1)S(1)}, bf16[1280,7168]{1,0:T(8,128)(2,1)}, u32[]{:S(2)}) copy-start(bf16[1280,7168]{1,0:T(8,128)(2,1)} %reshape.78) | copy-start | bytes 55050244
  407.0 14.4 %collective-permute-start.1 = (bf16[128,5,7168]{2,0,1:T(8,128)(2,1)S(1)}, bf16[128,5,7168]{2,0,1:T(8,128)(2,1)S(1)}, u32[]{:S(2)}, u32[]{:S(2)}) collective-permute-start(bf16[128,5,7168]{2,0,1:T(8,128)(2,1)S(1)} %copy.31), channel_id=1, source_target_pairs={{0,1},{1,0},{2,3},{3,2},{4,5},{5,4},{6,7},{7,6},{8,9},{9,8},{10,11... | collective-permute-start | bytes 27525128 | tf_op jit(solution)/shard_map/ppermute | solution.py:8
  432.4 9.5 %copy-start.4 = (s32[64,8]{1,0:T(8,128)S(1)}, s32[64,8]{1,0:T(8,128)}, u32[]{:S(2)}) copy-start(s32[64,8]{1,0:T(8,128)} %get-tuple-element.9) | copy-start | bytes 6148
  432.4 9.6 %copy-start.7 = (f32[64,8]{0,1:T(8,128)S(1)}, f32[64,8]{0,1:T(8,128)}, u32[]{:S(2)}) copy-start(f32[64,8]{0,1:T(8,128)} %param.8) | copy-start | bytes 6148
  432.4 9.6 %copy-start.6 = (s32[512]{0:T(512)S(1)}, s32[512]{0:T(512)}, u32[]{:S(2)}) copy-start(s32[512]{0:T(512)} %copy-done.5) | copy-start | bytes 6148
  432.4 209.2 %all-to-all-start.1 = ((bf16[128,5,7168]{2,1,0:T(8,128)(2,1)}), bf16[128,5,7168]{2,1,0:T(8,128)(2,1)}, u32[]{:S(2)}, u32[]{:S(2)}) async-start(bf16[128,5,7168]{2,1,0:T(8,128)(2,1)} %add_convert_fusion), calls=%async_computation.1 | async-start | bytes 29360128 | tf_op jit(solution)/shard_map/all_to_all | solution.py:16
  656.7 28.7 %copy-start.1 = (bf16[64,7168]{1,0:T(8,128)(2,1)S(1)}, bf16[64,7168]{1,0:T(8,128)(2,1)}, u32[]{:S(2)}) copy-start(bf16[64,7168]{1,0:T(8,128)(2,1)} %param.6) | copy-start | bytes 2752516
where the time goes:
time: 693 us; the launch traced here: 686 us
  waiting for transfers between devices  228 us (33%)
  blocking collectives  175 us (25%)
  local copies, waits for them, and re-layouts  154 us (22%)
  other arithmetic  66.2 us (10%)
  matrix products  51.5 us (7%)
  starting transfers between devices  10 us (1%)
    all_to_all x1, waiting for transfers between devices, return_rows(): lax.all_to_all(finished, ('group', 'local'), split_axis=0, concat_axis=0,...  199 us
    all_to_all x1, blocking collectives, send_rows(): lax.all_to_all(outgoing, ('group', 'local'), split_axis=0, concat_axis=0,...  175 us
    dynamic_slice x2, local copies, waits for them, and re-layouts, local(): lax.dynamic_slice_in_dim(partial_out, (1 - share) * halfcap, halfcap, 1)  39.3 us
    ppermute x2, waiting for transfers between devices, from_partner(): lax.ppermute(x, axis, [(i, i ^ 1 << stride) for i in range(lax.axis_size(...  28.7 us
    reshape x1, local copies, waits for them, and re-layouts, local(): rows_in = arrived.reshape(-1, width)  28.3 us
    reshape x1, local copies, waits for them, and re-layouts, local(): partial_out = partial_out.reshape(devices, capacity, width)  28.2 us
    select_n x1, other arithmetic, local(): leading = jnp.where(share == 0, raw, theirs)  22.3 us
    concatenate x1, other arithmetic, local(): arrived = jnp.concatenate([leading, trailing], axis=1)  20.5 us
  transfers between devices with their start and end apart: 3, of which 3 were waited for; matrix products, arithmetic and copies ran while one was open for 0% of the time, Pallas kernels for 0%

commit v1 on v0

v1 whole, which is shorter than its diff:
```python
import functools

import jax
import jax.numpy as jnp
from jax import lax
from jax.experimental import pallas as pl
from jax.experimental.pallas import tpu as pltpu
from jax.sharding import PartitionSpec as P

AXES = ("group", "local")
PARTS = 8
TILE = 32 * PARTS
SLOTS = (5,)
F32 = jnp.float32
BF16 = jnp.bfloat16


def quotient(value, by, most):
    shift = 0
    while True:
        factor = (1 << shift) // by + 1
        if factor * most < 1 << 31 and all(v * factor >> shift == v // by for v in range(most + 1)):
            return lax.shift_right_logical(value * factor, shift)
        shift += 1


def iota(shape, dim):
    return lax.broadcasted_iota(jnp.int32, shape, dim)


def expert_and_rank(row, slots, first, half, most):
    device = quotient(row, slots, most)
    slot = row - device * slots
    return lax.shift_right_logical(device, 1), (device & 1) * half + first + slot


def to_parts(dtype=BF16):
    p, q = iota((TILE, TILE), 0), iota((TILE, TILE), 1)
    return ((p & 31) * PARTS + (p >> 5) == q).astype(F32).astype(dtype)


def to_rows(dtype=BF16):
    p, q = iota((TILE, TILE), 0), iota((TILE, TILE), 1)
    return ((q & 31) * PARTS + (q >> 5) == p).astype(F32).astype(dtype)


def dot(a, b):
    return jnp.dot(a, b, preferred_element_type=F32)


def pack_body(slots, first, half, experts, routes_ref, tokens_ref, out_ref, codes_ref, tok_ref):
    rows, width = out_ref.shape
    toks = tokens_ref.shape[0]
    step = pl.program_id(0)

    @pl.when(step == 0)
    def _():
        names = iota((experts, toks), 0)
        hits = jnp.zeros((experts, toks), F32)
        for k in range(routes_ref.shape[0]):
            hits = hits + (routes_ref[k : k + 1, :] == names).astype(F32)
        before = (iota((toks, toks), 0) < iota((toks, toks), 1)).astype(F32).astype(BF16)
        earlier = dot(hits.astype(BF16), before)
        codes = (hits * (earlier + 1.0)).astype(BF16)
        wide = (toks, PARTS * toks)
        spread = ((iota(wide, 1) & (toks - 1)) == iota(wide, 0)).astype(F32).astype(BF16)
        codes_ref[...] = dot(codes, spread).astype(BF16)
        for s in range(PARTS):
            tok_ref[s * toks : (s + 1) * toks, :] = tokens_ref[:, s * width : (s + 1) * width]

    most = pl.num_programs(0) * rows // PARTS
    row = step * rows + iota((rows, 1), 0)
    expert, rank = expert_and_rank(row >> 3, slots, first, half, 1024)
    del most
    named = (iota((rows, experts), 1) == expert).astype(F32).astype(BF16)
    found = dot(named, codes_ref[...])
    wide = (rows, PARTS * toks)
    want = jnp.where((iota(wide, 1) >> 6) == (row & (PARTS - 1)), (rank + 1).astype(F32), -1.0)
    picks = jnp.where(found == want, 1.0, 0.0).astype(BF16)
    out_ref[...] = dot(picks, tok_ref[...]).astype(BF16)


def pack(routes_t, tokens, slots, first, half, devices):
    toks, width = tokens.shape
    part = width // PARTS
    rows = devices * slots * PARTS
    block = 512
    experts = devices // 2
    return pl.pallas_call(
        functools.partial(pack_body, slots, first, half, experts),
        grid=(rows // block,),
        out_shape=jax.ShapeDtypeStruct((rows, part), BF16),
        in_specs=[
            pl.BlockSpec(routes_t.shape, lambda i: (0, 0)),
            pl.BlockSpec(tokens.shape, lambda i: (0, 0)),
        ],
        out_specs=pl.BlockSpec((block, part), lambda i: (i, 0)),
        scratch_shapes=[
            pltpu.VMEM((experts, PARTS * toks), BF16),
            pltpu.VMEM((PARTS * toks, part), BF16),
        ],
        compiler_params=pltpu.CompilerParams(vmem_limit_bytes=32 << 20),
        cost_estimate=pl.CostEstimate(
            flops=2 * rows * PARTS * toks * part, bytes_accessed=2 * rows * part, transcendentals=0
        ),
        name="pack",
    )(routes_t, tokens)


def ffn_body(blocks, rows_in, ga, gb, ua, ub, da, db, out_ref, parts, acc, hidden):
    step = pl.program_id(0)
    block, part = rows_in.shape
    tiles = block // TILE
    half = hidden.shape[1] // 2

    @pl.when(step < blocks)
    def _():
        order = to_parts()
        for t in range(tiles):
            turned = dot(order, rows_in[t * TILE : (t + 1) * TILE, :]).astype(BF16)
            at = pl.multiple_of((step * tiles + t) * 32, 32)
            for s in range(PARTS):
                parts[s, pl.ds(at, 32), :] = turned[s * 32 : (s + 1) * 32, :]

    def add(first):
        x = parts[jnp.where(first, 0, step - blocks)]
        for k, w in enumerate((ga, gb, ua, ub)):
            value = dot(x, w[0])
            acc[k] = value if first else acc[k] + value

    @pl.when(step == blocks)
    def _():
        add(True)

    @pl.when((step > blocks) & (step < blocks + PARTS))
    def _():
        add(False)

    @pl.when(step == blocks + PARTS - 1)
    def _():
        for k in range(2):
            gate = acc[k]
            value = gate / (1.0 + jnp.exp(-gate)) * acc[2 + k]
            hidden[:, k * half : (k + 1) * half] = value.astype(BF16)

    @pl.when((step >= blocks + PARTS) & (step < blocks + 2 * PARTS))
    def _():
        value = dot(hidden[:, :half], da[0]) + dot(hidden[:, half:], db[0])
        parts[step - blocks - PARTS] = value.astype(BF16)

    @pl.when(step >= blocks + 2 * PARTS)
    def _():
        order = to_rows()
        for t in range(tiles):
            at = pl.multiple_of(((step - blocks - 2 * PARTS) * tiles + t) * 32, 32)
            stacked = jnp.concatenate([parts[s, pl.ds(at, 32), :] for s in range(PARTS)], axis=0)
            out_ref[t * TILE : (t + 1) * TILE, :] = dot(order, stacked).astype(BF16)


def ffn(rows_in, gate, gate_other, up, up_other, down, down_other):
    total, part = rows_in.shape
    rows = total // PARTS
    half = gate.shape[2]
    block = 512
    blocks = total // block
    last = PARTS - 1
    into = lambda i: (0, jnp.clip(i - blocks, 0, last), 0)
    outof = lambda i: (0, 0, jnp.clip(i - blocks - PARTS, 0, last))
    up_spec = pl.BlockSpec((1, part, half), into)
    down_spec = pl.BlockSpec((1, half, part), outof)
    return pl.pallas_call(
        functools.partial(ffn_body, blocks),
        grid=(2 * blocks + 2 * PARTS,),
        out_shape=jax.ShapeDtypeStruct((total, part), BF16),
        in_specs=[
            pl.BlockSpec((block, part), lambda i: (jnp.minimum(i, blocks - 1), 0)),
            up_spec,
            up_spec,
            up_spec,
            up_spec,
            down_spec,
            down_spec,
        ],
        out_specs=pl.BlockSpec((block, part), lambda i: (jnp.maximum(i - blocks - 2 * PARTS, 0), 0)),
        scratch_shapes=[
            pltpu.VMEM((PARTS, rows, part), BF16),
            pltpu.VMEM((4, rows, half), F32),
            pltpu.VMEM((rows, 2 * half), BF16),
        ],
        compiler_params=pltpu.CompilerParams(vmem_limit_bytes=48 << 20),
        cost_estimate=pl.CostEstimate(
            flops=2 * rows * part * PARTS * half * 6,
            bytes_accessed=4 * total * part + 12 * part * PARTS * half,
            transcendentals=rows * 2 * half,
        ),
        name="experts",
    )(rows_in, gate, gate_other, up, up_other, down, down_other)


def mix_body(slots, first, half, experts, blocks, with_sum, *refs):
    if with_sum:
        routes_ref, gates_ref, rows_ref, sum_ref, out_ref, parts = refs
    else:
        routes_ref, gates_ref, rows_ref, out_ref, parts = refs
    step = pl.program_id(0)
    block, part = rows_ref.shape
    tiles = block // TILE
    toks = routes_ref.shape[0]
    order = to_parts()
    for t in range(tiles):
        turned = dot(order, rows_ref[t * TILE : (t + 1) * TILE, :]).astype(BF16)
        at = pl.multiple_of((step * tiles + t) * 32, 32)
        for s in range(PARTS):
            parts[s, pl.ds(at, 32), :] = turned[s * 32 : (s + 1) * 32, :]

    @pl.when(step == blocks - 1)
    def _():
        rows = parts.shape[1]
        names = iota((toks, experts), 1)
        hits = jnp.zeros((toks, experts), F32)
        weight = jnp.zeros((toks, experts), F32)
        for k in range(routes_ref.shape[1]):
            hit = (routes_ref[:, k : k + 1] == names).astype(F32)
            hits = hits + hit
            weight = weight + hit * gates_ref[:, k : k + 1]
        before = (iota((toks, toks), 1) < iota((toks, toks), 0)).astype(F32).astype(BF16)
        codes = (hits * (dot(before, hits.astype(BF16)) + 1.0)).astype(BF16)
        high = weight.astype(BF16)
        low = (weight - high.astype(F32)).astype(BF16)
        expert, rank = expert_and_rank(iota((1, rows), 1), slots, first, half, 1024)
        spread = (iota((experts, rows), 0) == expert).astype(F32).astype(BF16)
        here = dot(codes, spread) == (rank + 1).astype(F32)
        high = jnp.where(here, dot(high, spread), 0.0).astype(BF16)
        low = jnp.where(here, dot(low, spread), 0.0).astype(BF16)
        both = jnp.concatenate([high, low], axis=0)
        for s in range(PARTS):
            value = dot(both, parts[s])
            value = value[:toks] + value[toks:]
            at = slice(s * part, (s + 1) * part)
            if with_sum:
                value = value + sum_ref[:, at]
            out_ref[:, at] = value.astype(out_ref.dtype)


def mix(routes, gates, rows_in, so_far, slots, first, half, devices, dtype):
    total, part = rows_in.shape
    toks = routes.shape[0]
    block = 512
    blocks = total // block
    whole = lambda i: (0, 0)
    extra = () if so_far is None else (so_far,)
    return pl.pallas_call(
        functools.partial(mix_body, slots, first, half, devices // 2, blocks, bool(extra)),
        grid=(blocks,),
        out_shape=jax.ShapeDtypeStruct((toks, part * PARTS), dtype),
        in_specs=[
            pl.BlockSpec(routes.shape, whole),
            pl.BlockSpec(gates.shape, whole),
            pl.BlockSpec((block, part), lambda i: (i, 0)),
        ]
        + [pl.BlockSpec(x.shape, whole) for x in extra],
        out_specs=pl.BlockSpec((toks, part * PARTS), whole),
        scratch_shapes=[pltpu.VMEM((PARTS, total // PARTS, part), BF16)],
        compiler_params=pltpu.CompilerParams(vmem_limit_bytes=32 << 20),
        cost_estimate=pl.CostEstimate(
            flops=2 * total * TILE * part, bytes_accessed=2 * total * part, transcendentals=0
        ),
        name="mix",
    )(routes, gates, rows_in, *extra)


def exchange(rows, devices):
    part = rows.shape[1]
    rows = rows.reshape(devices, -1, part)
    return lax.all_to_all(rows, AXES, split_axis=0, concat_axis=0, tiled=True).reshape(-1, part)


def local(tokens, routes, gates, gate_weight, up_weight, down_weight):
    devices = lax.axis_size("group") * lax.axis_size("local")
    half = sum(SLOTS)
    swap = [(i, i ^ 1) for i in range(lax.axis_size("local"))]
    others = [lax.ppermute(w, "local", swap) for w in (gate_weight, up_weight, down_weight)]
    routes_t = routes.T
    firsts = [sum(SLOTS[:n]) for n in range(len(SLOTS))]
    packed = [pack(routes_t, tokens, n, f, half, devices) for n, f in zip(SLOTS, firsts)]
    arrived = [exchange(p, devices) for p in packed]
    done = [
        ffn(a, gate_weight, others[0], up_weight, others[1], down_weight, others[2])
        for a in arrived
    ]
    back = [exchange(d, devices) for d in done]
    mixed = None
    for at, (n, f) in enumerate(zip(SLOTS, firsts)):
        dtype = BF16 if at == len(SLOTS) - 1 else F32
        mixed = mix(routes, gates, back[at], mixed, n, f, half, devices, dtype)
    return mixed


def solution(mesh):
    placed = (
        P(AXES, None),
        P(AXES, None),
        P(AXES, None),
        P(AXES, None, None),
        P(AXES, None, None),
        P(AXES, None, None),
    )
    return jax.shard_map(
        local, mesh=mesh, in_specs=placed, out_specs=P(AXES, None), check_vma=False
    )
```

time: 693 us -> 335 us (0.48)
  blocking collectives: 175 us -> 0 us
  local copies, waits for them, and re-layouts: 154 us -> 5.58 us
  Pallas kernels: 0 us -> 77.4 us
  other arithmetic: 66.2 us -> 0 us
  matrix products: 51.5 us -> 0 us
  starting transfers between devices: 10 us -> 21.9 us
    all_to_all x1 -> x0, blocking collectives: 175 us -> none  [send_rows(): lax.all_to_all(outgoing, ('group', 'local'), split_axis=0, concat_axis=0,...]
    reshape x4 -> x0, local copies, waits for them, and re-layouts: 86.3 us -> none  [the longest x1 28.3 us: local(): rows_in = arrived.reshape(-1, width)]
    pallas_call x0 -> x3, Pallas kernels: none -> 77.4 us  [the longest x1 55.9 us: ffn(): pl.pallas_call(functools.partial(ffn_body, blocks), grid=(2 * blocks + 2...]
    dot_general x4 -> x0, matrix products: 51.5 us -> none  [the longest x1 16.6 us: local(): jnp.dot(hidden, down_weight[0], preferred_element_type=jnp.float32)]
    dynamic_slice x2 -> x0, local copies, waits for them, and re-layouts: 39.3 us -> none  [local(): lax.dynamic_slice_in_dim(partial_out, (1 - share) * halfcap, halfcap, 1)]
    select_n x2 -> x0, other arithmetic: 22.4 us -> none  [the longest x1 22.3 us: local(): leading = jnp.where(share == 0, raw, theirs)]
    concatenate x1 -> x0, other arithmetic: 20.5 us -> none  [local(): arrived = jnp.concatenate([leading, trailing], axis=1)]
    gather x1 -> x0, local copies, waits for them, and re-layouts: 18.9 us -> none  [local(): picked = returned[places].reshape(tok_rows, chosen, width)]
  transfers between devices with their start and end apart: 3 -> 5, of which waited for: 3 -> 5; matrix products, arithmetic and copies ran while one was open for 0% -> 0% of each run, Pallas kernels for 0% -> 0%
where the time goes in v1:
time: 335 us; the launch traced here: 333 us
  waiting for transfers between devices  228 us (68%)
  Pallas kernels  77.4 us (23%)
  starting transfers between devices  21.9 us (7%)
  local copies, waits for them, and re-layouts  5.58 us (2%)
    all_to_all x2, waiting for transfers between devices, exchange(): lax.all_to_all(rows, AXES, split_axis=0, concat_axis=0, tiled=True)  196 us
    pallas_call x1, Pallas kernels, ffn(): pl.pallas_call(functools.partial(ffn_body, blocks), grid=(2 * blocks + 2...  55.9 us
    ppermute x3, waiting for transfers between devices, local(): lax.ppermute(w, 'local', swap)  32.3 us
    all_to_all x2, starting transfers between devices, exchange(): lax.all_to_all(rows, AXES, split_axis=0, concat_axis=0, tiled=True)  21.1 us
    pallas_call x1, Pallas kernels, mix(): pl.pallas_call(functools.partial(mix_body, slots, first, half, devices //...  12.1 us
    pallas_call x1, Pallas kernels, pack(): pl.pallas_call(functools.partial(pack_body, slots, first, half, experts),...  9.39 us
  transfers between devices with their start and end apart: 5, of which 5 were waited for; matrix products, arithmetic and copies ran while one was open for 0% of the time, Pallas kernels for 0%

profile of v1, /device:TPU:12, one launch (start us, length us, event | category | flops | bytes accessed | tf_op | source)
XLA Modules:
  0.0 333.0 jit_solution(3912770730969194176)
XLA Ops:
  0.0 0.0 copy-start.1
  0.0 0.7 copy-done.1
  0.7 0.0 copy-start.3
  0.7 1.2 copy-done.3
  1.9 9.4 %pack.1 = bf16[5120,896]{1,0:T(8,128)(2,1)S(1)} custom-call(s32[8,64]{1,0:T(8,128)S(1)} %bitcast.6, bf16[64,7168]{1,0:T(8,128)(2,1)S(1)} %copy-done.3), custom_call_target="tpu_custom_call" | custom-call | flops 4697620480 | bytes 9175040 | tf_op jit(solution)/shard_map/pack/pallas_call | solution.py:89
  11.3 0.0 copy-start
  11.3 3.5 %copy-done = bf16[5120,896]{1,0:T(8,128)(2,1)} copy-done((bf16[5120,896]{1,0:T(8,128)(2,1)}, bf16[5120,896]{1,0:T(8,128)(2,1)S(1)}, u32[]{:S(2)}) %copy-start) | copy-done | bytes 9175064
  14.8 10.8 %all-to-all-start = ((bf16[128,40,896]{2,1,0:T(8,128)(2,1)}), bf16[128,40,896]{2,1,0:T(8,128)(2,1)}, u32[]{:S(2)}, u32[]{:S(2)}) async-start(bf16[128,40,896]{2,1,0:T(8,128)(2,1)} %bitcast.5), calls=%async_computation | async-start | bytes 18350080 | tf_op jit(solution)/shard_map/all_to_all | solution.py:275
  25.6 0.2 collective-permute-start
  25.8 0.4 collective-permute-start.1
  26.2 0.1 collective-permute-start.2
  26.4 11.3 %collective-permute-done.gb = bf16[1,7168,512]{2,1,0:T(8,128)(2,1)} collective-permute-done((bf16[1,7168,512]{2,1,0:T(8,128)(2,1)}, bf16[1,7168,512]{2,1,0:T(8,128)(2,1)}, u32[]{:S(2)}, u32[]{:S(2)}) %collective-permute-start) | collective-permute-done | bytes 7340064 | tf_op jit(solution)/shard_map/ppermute | solution.py:282
  37.7 10.5 %collective-permute-done.1.ub = bf16[1,7168,512]{2,1,0:T(8,128)(2,1)} collective-permute-done((bf16[1,7168,512]{2,1,0:T(8,128)(2,1)}, bf16[1,7168,512]{2,1,0:T(8,128)(2,1)}, u32[]{:S(2)}, u32[]{:S(2)}) %collective-permute-start.1) | collective-permute-done | bytes 7340064 | tf_op jit(solution)/shard_map/ppermute | solution.py:282
  48.2 10.5 %collective-permute-done.2.db = bf16[1,512,7168]{2,1,0:T(8,128)(2,1)} collective-permute-done((bf16[1,512,7168]{2,1,0:T(8,128)(2,1)}, bf16[1,512,7168]{2,1,0:T(8,128)(2,1)}, u32[]{:S(2)}, u32[]{:S(2)}) %collective-permute-start.2) | collective-permute-done | bytes 7340064 | tf_op jit(solution)/shard_map/ppermute | solution.py:282
  58.7 81.5 %all-to-all-done = bf16[128,40,896]{2,1,0:T(8,128)(2,1)} async-done(((bf16[128,40,896]{2,1,0:T(8,128)(2,1)}), bf16[128,40,896]{2,1,0:T(8,128)(2,1)}, u32[]{:S(2)}, u32[]{:S(2)}) %all-to-all-start) | async-done | bytes 9175072 | tf_op jit(solution)/shard_map/all_to_all | solution.py:275
  140.2 55.9 %experts.1 = bf16[5120,896]{1,0:T(8,128)(2,1)} custom-call(bf16[5120,896]{1,0:T(8,128)(2,1)} %bitcast.2.rows_in, bf16[1,7168,512]{2,1,0:T(8,128)(2,1)} %ga.1, bf16[1,7168,512]{2,1,0:T(8,128)(2,1)} %collective-permute-done.gb, bf16[1,7168,512]{2,1,0:T(8,128)(2,1)} %ua.1, bf16[1,7168,512]{2,1,0:T(8,128)(2,1)} %collective-permute-done.1.ub, ...), custom_call_target="tpu_custom_call" | custom-call | flops 28185722880 | bytes 62390272 | tf_op jit(solution)/shard_map/experts/pallas_call | solution.py:171
  196.1 0.0 copy-start.2
  196.1 0.0 copy-start.4
  196.1 10.3 %all-to-all-start.1 = ((bf16[128,40,896]{2,1,0:T(8,128)(2,1)}), bf16[128,40,896]{2,1,0:T(8,128)(2,1)}, u32[]{:S(2)}, u32[]{:S(2)}) async-start(bf16[128,40,896]{2,1,0:T(8,128)(2,1)} %bitcast.7), calls=%async_computation.1 | async-start | bytes 18350080 | tf_op jit(solution)/shard_map/all_to_all | solution.py:275
  206.4 0.0 copy-done.2
  206.4 0.1 copy.7.refs_0_
  206.5 0.0 copy-done.4
  206.5 0.1 copy.8.refs_1_
  206.6 114.4 %all-to-all-done.1 = bf16[128,40,896]{2,1,0:T(8,128)(2,1)} async-done(((bf16[128,40,896]{2,1,0:T(8,128)(2,1)}), bf16[128,40,896]{2,1,0:T(8,128)(2,1)}, u32[]{:S(2)}, u32[]{:S(2)}) %all-to-all-start.1) | async-done | bytes 9175072 | tf_op jit(solution)/shard_map/all_to_all | solution.py:275
  321.0 12.1 %mix.1 = bf16[64,7168]{1,0:T(8,128)(2,1)} custom-call(s32[64,8]{1,0:T(8,128)S(1)} %copy.7.refs_0_, f32[64,8]{1,0:T(8,128)S(1)} %copy.8.refs_1_, bf16[5120,896]{1,0:T(8,128)(2,1)} %bitcast.4.refs_2_), custom_call_target="tpu_custom_call" | custom-call | flops 2348810240 | bytes 9175040 | tf_op jit(solution)/shard_map/mix/pallas_call | solution.py:252
Async XLA Ops:
  0.0 0.7 copy-start.1
  0.7 1.2 copy-start.3
  11.3 3.5 %copy-start = (bf16[5120,896]{1,0:T(8,128)(2,1)}, bf16[5120,896]{1,0:T(8,128)(2,1)S(1)}, u32[]{:S(2)}) copy-start(bf16[5120,896]{1,0:T(8,128)(2,1)S(1)} %pack.1) | copy-start | bytes 27525124
  14.8 125.3 %all-to-all-start = ((bf16[128,40,896]{2,1,0:T(8,128)(2,1)}), bf16[128,40,896]{2,1,0:T(8,128)(2,1)}, u32[]{:S(2)}, u32[]{:S(2)}) async-start(bf16[128,40,896]{2,1,0:T(8,128)(2,1)} %bitcast.5), calls=%async_computation | async-start | bytes 18350080 | tf_op jit(solution)/shard_map/all_to_all | solution.py:275
  25.6 12.1 %collective-permute-start = (bf16[1,7168,512]{2,1,0:T(8,128)(2,1)}, bf16[1,7168,512]{2,1,0:T(8,128)(2,1)}, u32[]{:S(2)}, u32[]{:S(2)}) collective-permute-start(bf16[1,7168,512]{2,1,0:T(8,128)(2,1)} %ga.1), channel_id=1, source_target_pairs={{0,1},{1,0},{2,3},{3,2},{4,5},{5,4},{6,7},{7,6},{8,9},{9,8},{10,11... | collective-permute-start | bytes 22020104 | tf_op jit(solution)/shard_map/ppermute | solution.py:282
  25.8 22.3 %collective-permute-start.1 = (bf16[1,7168,512]{2,1,0:T(8,128)(2,1)}, bf16[1,7168,512]{2,1,0:T(8,128)(2,1)}, u32[]{:S(2)}, u32[]{:S(2)}) collective-permute-start(bf16[1,7168,512]{2,1,0:T(8,128)(2,1)} %ua.1), channel_id=1, source_target_pairs={{0,1},{1,0},{2,3},{3,2},{4,5},{5,4},{6,7},{7,6},{8,9},{9,8},{10,11... | collective-permute-start | bytes 22020104 | tf_op jit(solution)/shard_map/ppermute | solution.py:282
  26.2 32.5 %collective-permute-start.2 = (bf16[1,512,7168]{2,1,0:T(8,128)(2,1)}, bf16[1,512,7168]{2,1,0:T(8,128)(2,1)}, u32[]{:S(2)}, u32[]{:S(2)}) collective-permute-start(bf16[1,512,7168]{2,1,0:T(8,128)(2,1)} %da.1), channel_id=1, source_target_pairs={{0,1},{1,0},{2,3},{3,2},{4,5},{5,4},{6,7},{7,6},{8,9},{9,8},{10,11... | collective-permute-start | bytes 22020104 | tf_op jit(solution)/shard_map/ppermute | solution.py:282
  196.1 10.3 %copy-start.2 = (s32[64,8]{0,1:T(8,128)S(1)}, s32[64,8]{0,1:T(8,128)}, u32[]{:S(2)}) copy-start(s32[64,8]{0,1:T(8,128)} %param.7) | copy-start | bytes 6148
  196.1 10.4 %copy-start.4 = (f32[64,8]{0,1:T(8,128)S(1)}, f32[64,8]{0,1:T(8,128)}, u32[]{:S(2)}) copy-start(f32[64,8]{0,1:T(8,128)} %param.8) | copy-start | bytes 6148
  196.1 124.9 %all-to-all-start.1 = ((bf16[128,40,896]{2,1,0:T(8,128)(2,1)}), bf16[128,40,896]{2,1,0:T(8,128)(2,1)}, u32[]{:S(2)}, u32[]{:S(2)}) async-start(bf16[128,40,896]{2,1,0:T(8,128)(2,1)} %bitcast.7), calls=%async_computation.1 | async-start | bytes 18350080 | tf_op jit(solution)/shard_map/all_to_all | solution.py:275

commit v2 on v1

v2 whole, which is shorter than its diff:
```python
import functools

import jax
import jax.numpy as jnp
from jax import lax
from jax.experimental import pallas as pl
from jax.experimental.pallas import tpu as pltpu
from jax.sharding import Mesh, PartitionSpec as P

AXES = ("group", "chip", "core")
CHIPS = ("group", "chip")
PARTS = 4
ROWS = 64
TILE = ROWS * PARTS
SLOTS = (6, 4)
BLOCK = 512
VMEM = 60 << 20
F32 = jnp.float32
BF16 = jnp.bfloat16


def quotient(value, by, most):
    shift = 0
    while True:
        factor = (1 << shift) // by + 1
        if factor * most < 1 << 31 and all(v * factor >> shift == v // by for v in range(most + 1)):
            return lax.shift_right_logical(value * factor, shift)
        shift += 1


def iota(shape, dim):
    return lax.broadcasted_iota(jnp.int32, shape, dim)


def expert_and_rank(row, slots, first):
    expert = quotient(row, slots, 1024)
    return expert, row - expert * slots + first


def order(rows_first):
    p, q = iota((TILE, TILE), rows_first), iota((TILE, TILE), 1 - rows_first)
    return (lax.rem(p, ROWS) * PARTS + lax.div(p, ROWS) == q).astype(F32).astype(BF16)


def dot(a, b):
    return jnp.dot(a, b, preferred_element_type=F32)


def pack_body(slots, first, experts, routes_ref, tokens_ref, out_ref, codes_ref, tok_ref):
    rows, width = out_ref.shape
    toks = tokens_ref.shape[0]
    step = pl.program_id(0)

    @pl.when(step == 0)
    def _():
        names = iota((experts, toks), 0)
        hits = jnp.zeros((experts, toks), F32)
        for k in range(routes_ref.shape[0]):
            hits = hits + (routes_ref[k : k + 1, :] == names).astype(F32)
        before = (iota((toks, toks), 0) < iota((toks, toks), 1)).astype(F32).astype(BF16)
        earlier = dot(hits.astype(BF16), before)
        codes = (hits * (earlier + 1.0)).astype(BF16)
        wide = (toks, PARTS * toks)
        spread = ((iota(wide, 1) & (toks - 1)) == iota(wide, 0)).astype(F32).astype(BF16)
        codes_ref[...] = dot(codes, spread).astype(BF16)
        for s in range(PARTS):
            tok_ref[s * toks : (s + 1) * toks, :] = tokens_ref[:, s * width : (s + 1) * width]

    row = step * rows + iota((rows, 1), 0)
    expert, rank = expert_and_rank(lax.div(row, PARTS), slots, first)
    named = (iota((rows, experts), 1) == expert).astype(F32).astype(BF16)
    found = dot(named, codes_ref[...])
    wide = (rows, PARTS * toks)
    want = jnp.where(lax.div(iota(wide, 1), toks) == lax.rem(row, PARTS), (rank + 1).astype(F32), -1.0)
    picks = jnp.where(found == want, 1.0, 0.0).astype(BF16)
    out_ref[...] = dot(picks, tok_ref[...]).astype(BF16)


def pack(routes_t, tokens, slots, first, experts):
    toks, width = tokens.shape
    part = width // PARTS
    rows = experts * slots * PARTS
    block = BLOCK
    return pl.pallas_call(
        functools.partial(pack_body, slots, first, experts),
        grid=(rows // block,),
        out_shape=jax.ShapeDtypeStruct((rows, part), BF16),
        in_specs=[
            pl.BlockSpec(routes_t.shape, lambda i: (0, 0)),
            pl.BlockSpec(tokens.shape, lambda i: (0, 0)),
        ],
        out_specs=pl.BlockSpec((block, part), lambda i: (i, 0)),
        scratch_shapes=[
            pltpu.VMEM((experts, PARTS * toks), BF16),
            pltpu.VMEM((PARTS * toks, part), BF16),
        ],
        compiler_params=pltpu.CompilerParams(vmem_limit_bytes=VMEM),
        cost_estimate=pl.CostEstimate(
            flops=2 * rows * PARTS * toks * part, bytes_accessed=2 * rows * part, transcendentals=0
        ),
        name="pack",
    )(routes_t, tokens)


def split(step, rows_ref, parts):
    apart = order(0)
    tiles = rows_ref.shape[0] // TILE
    for t in range(tiles):
        turned = dot(apart, rows_ref[t * TILE : (t + 1) * TILE, :]).astype(BF16)
        at = pl.multiple_of((step * tiles + t) * ROWS, ROWS)
        for s in range(PARTS):
            parts[s, pl.ds(at, ROWS), :] = turned[s * ROWS : (s + 1) * ROWS, :]


def ffn_body(blocks, rows_in, ga, gb, ua, ub, da, db, out_ref, parts, acc, hidden):
    step = pl.program_id(0)
    block = rows_in.shape[0]
    half = hidden.shape[1] // 2

    @pl.when(step < blocks)
    def _():
        split(step, rows_in, parts)

    def add(first):
        x = parts[jnp.where(first, 0, step - blocks)]
        for k, w in enumerate((ga, gb, ua, ub)):
            value = dot(x, w[0])
            acc[k] = value if first else acc[k] + value

    @pl.when(step == blocks)
    def _():
        add(True)

    @pl.when((step > blocks) & (step < blocks + PARTS))
    def _():
        add(False)

    @pl.when(step == blocks + PARTS - 1)
    def _():
        for k in range(2):
            gate = acc[k]
            value = gate / (1.0 + jnp.exp(-gate)) * acc[2 + k]
            hidden[:, k * half : (k + 1) * half] = value.astype(BF16)

    @pl.when((step >= blocks + PARTS) & (step < blocks + 2 * PARTS))
    def _():
        halves = [dot(hidden[:, :half], da[0]), dot(hidden[:, half:], db[0])]
        own, other = (v.astype(BF16).astype(F32) for v in halves)
        parts[step - blocks - PARTS] = (own + other).astype(BF16)

    @pl.when(step >= blocks + 2 * PARTS)
    def _():
        back = order(1)
        tiles = block // TILE
        for t in range(tiles):
            at = pl.multiple_of(((step - blocks - 2 * PARTS) * tiles + t) * ROWS, ROWS)
            stacked = jnp.concatenate([parts[s, pl.ds(at, ROWS), :] for s in range(PARTS)], axis=0)
            out_ref[t * TILE : (t + 1) * TILE, :] = dot(back, stacked).astype(BF16)


def ffn(rows_in, gate, gate_other, up, up_other, down, down_other):
    total, part = rows_in.shape
    rows = total // PARTS
    half = gate.shape[2]
    block = BLOCK
    blocks = total // block
    last = PARTS - 1
    into = lambda i: (0, jnp.clip(i - blocks, 0, last), 0)
    outof = lambda i: (0, 0, jnp.clip(i - blocks - PARTS, 0, last))
    up_spec = pl.BlockSpec((1, part, half), into)
    down_spec = pl.BlockSpec((1, half, part), outof)
    return pl.pallas_call(
        functools.partial(ffn_body, blocks),
        grid=(2 * blocks + 2 * PARTS,),
        out_shape=jax.ShapeDtypeStruct((total, part), BF16),
        in_specs=[
            pl.BlockSpec((block, part), lambda i: (jnp.minimum(i, blocks - 1), 0)),
            up_spec,
            up_spec,
            up_spec,
            up_spec,
            down_spec,
            down_spec,
        ],
        out_specs=pl.BlockSpec((block, part), lambda i: (jnp.maximum(i - blocks - 2 * PARTS, 0), 0)),
        scratch_shapes=[
            pltpu.VMEM((PARTS, rows, part), BF16),
            pltpu.VMEM((4, rows, half), F32),
            pltpu.VMEM((rows, 2 * half), BF16),
        ],
        compiler_params=pltpu.CompilerParams(vmem_limit_bytes=VMEM),
        cost_estimate=pl.CostEstimate(
            flops=2 * rows * part * PARTS * half * 6,
            bytes_accessed=4 * total * part + 12 * part * PARTS * half,
            transcendentals=rows * 2 * half,
        ),
        name="experts",
    )(rows_in, gate, gate_other, up, up_other, down, down_other)


def mix_body(slots, first, experts, blocks, with_sum, *refs):
    if with_sum:
        routes_ref, gates_ref, rows_ref, sum_ref, out_ref, parts = refs
    else:
        routes_ref, gates_ref, rows_ref, out_ref, parts = refs
    step = pl.program_id(0)
    part = rows_ref.shape[1]
    toks = routes_ref.shape[0]
    split(step, rows_ref, parts)

    @pl.when(step == blocks - 1)
    def _():
        rows = parts.shape[1]
        names = iota((toks, experts), 1)
        hits = jnp.zeros((toks, experts), F32)
        weight = jnp.zeros((toks, experts), F32)
        for k in range(routes_ref.shape[1]):
            hit = (routes_ref[:, k : k + 1] == names).astype(F32)
            hits = hits + hit
            weight = weight + hit * gates_ref[:, k : k + 1]
        before = (iota((toks, toks), 1) < iota((toks, toks), 0)).astype(F32).astype(BF16)
        codes = (hits * (dot(before, hits.astype(BF16)) + 1.0)).astype(BF16)
        high = weight.astype(BF16)
        low = (weight - high.astype(F32)).astype(BF16)
        expert, rank = expert_and_rank(iota((1, rows), 1), slots, first)
        spread = (iota((experts, rows), 0) == expert).astype(F32).astype(BF16)
        here = dot(codes, spread) == (rank + 1).astype(F32)
        high = jnp.where(here, dot(high, spread), 0.0).astype(BF16)
        low = jnp.where(here, dot(low, spread), 0.0).astype(BF16)
        both = jnp.concatenate([high, low], axis=0)
        for s in range(PARTS):
            value = dot(both, parts[s])
            value = value[:toks] + value[toks:]
            at = slice(s * part, (s + 1) * part)
            if with_sum:
                value = value + sum_ref[:, at]
            out_ref[:, at] = value.astype(out_ref.dtype)


def mix(routes, gates, rows_in, so_far, slots, first, experts, dtype):
    total, part = rows_in.shape
    toks = routes.shape[0]
    block = BLOCK
    blocks = total // block
    whole = lambda i: (0, 0)
    extra = () if so_far is None else (so_far,)
    return pl.pallas_call(
        functools.partial(mix_body, slots, first, experts, blocks, bool(extra)),
        grid=(blocks,),
        out_shape=jax.ShapeDtypeStruct((toks, part * PARTS), dtype),
        in_specs=[
            pl.BlockSpec(routes.shape, whole),
            pl.BlockSpec(gates.shape, whole),
            pl.BlockSpec((block, part), lambda i: (i, 0)),
        ]
        + [pl.BlockSpec(x.shape, whole) for x in extra],
        out_specs=pl.BlockSpec((toks, part * PARTS), whole),
        scratch_shapes=[pltpu.VMEM((PARTS, total // PARTS, part), BF16)],
        compiler_params=pltpu.CompilerParams(vmem_limit_bytes=VMEM),
        cost_estimate=pl.CostEstimate(
            flops=2 * total * TILE * part, bytes_accessed=2 * total * part, transcendentals=0
        ),
        name="mix",
    )(routes, gates, rows_in, *extra)


def exchange(rows, experts):
    part = rows.shape[1]
    rows = rows.reshape(experts, -1, part)
    return lax.all_to_all(rows, CHIPS, split_axis=0, concat_axis=0, tiled=True).reshape(-1, part)


def local(tokens, routes, gates, gate_weight, up_weight, down_weight):
    experts = lax.axis_size("group") * lax.axis_size("chip")
    swap = [(0, 1), (1, 0)]
    others = [lax.ppermute(w, "core", swap) for w in (gate_weight, up_weight, down_weight)]
    routes_t = routes.T
    firsts = [sum(SLOTS[:n]) for n in range(len(SLOTS))]
    packed = [pack(routes_t, tokens, n, f, experts) for n, f in zip(SLOTS, firsts)]
    arrived = [exchange(p, experts) for p in packed]
    done = [
        ffn(a, gate_weight, others[0], up_weight, others[1], down_weight, others[2])
        for a in arrived
    ]
    back = [exchange(d, experts) for d in done]
    mixed = None
    for at, (n, f) in enumerate(zip(SLOTS, firsts)):
        dtype = BF16 if at == len(SLOTS) - 1 else F32
        mixed = mix(routes, gates, back[at], mixed, n, f, experts, dtype)
    return mixed


def solution(mesh):
    groups, members = mesh.devices.shape
    by_core = Mesh(mesh.devices.reshape(groups, members // 2, 2), AXES)
    placed = (
        P(AXES, None),
        P(AXES, None),
        P(AXES, None),
        P(AXES, None, None),
        P(AXES, None, None),
        P(AXES, None, None),
    )
    return jax.shard_map(
        local, mesh=by_core, in_specs=placed, out_specs=P(AXES, None), check_vma=False
    )
```

time: 335 us -> 276 us (0.82)
  waiting for transfers between devices: 228 us -> 148 us
  starting transfers between devices: 21.9 us -> 43.2 us
  local copies, waits for them, and re-layouts: 5.58 us -> 1.4 us
    all_to_all x2 -> x4, waiting for transfers between devices: 196 us -> 148 us  [exchange(): lax.all_to_all(rows, CHIPS, split_axis=0, concat_axis=0, tiled=True)]
    ppermute x3, waiting for transfers between devices: 32.3 us -> 0.01 us  [local(): lax.ppermute(w, 'core', swap)]
    all_to_all x2 -> x4, starting transfers between devices: 21.1 us -> 42.5 us  [exchange(): lax.all_to_all(rows, CHIPS, split_axis=0, concat_axis=0, tiled=True)]
    unnamed x12 -> x6, local copies, waits for them, and re-layouts: 5.58 us -> 1.4 us
    pallas_call x1 -> x2, Pallas kernels: 55.9 us -> 58 us  [ffn(): pl.pallas_call(functools.partial(ffn_body, blocks), grid=(2 * blocks + 2...]
    pallas_call x2 -> x4, Pallas kernels: 21.4 us -> 22.2 us  [the longest x2 12.4 us: mix(): pl.pallas_call(functools.partial(mix_body, slots, first, experts, blocks,...]
  transfers between devices with their start and end apart: 5 -> 7, of which waited for: 5 -> 4; matrix products, arithmetic and copies ran while one was open for 0% -> 1% of each run, Pallas kernels for 0% -> 25%
where the time goes in v2:
time: 276 us; the launch traced here: 273 us
  waiting for transfers between devices  148 us (54%)
  Pallas kernels  80.2 us (29%)
  starting transfers between devices  43.2 us (16%)
    all_to_all x4, waiting for transfers between devices, exchange(): lax.all_to_all(rows, CHIPS, split_axis=0, concat_axis=0, tiled=True)  148 us
    pallas_call x2, Pallas kernels, ffn(): pl.pallas_call(functools.partial(ffn_body, blocks), grid=(2 * blocks + 2...  58 us
    all_to_all x4, starting transfers between devices, exchange(): lax.all_to_all(rows, CHIPS, split_axis=0, concat_axis=0, tiled=True)  42.5 us
    pallas_call x2, Pallas kernels, mix(): pl.pallas_call(functools.partial(mix_body, slots, first, experts, blocks,...  12.4 us
    pallas_call x2, Pallas kernels, pack(): pl.pallas_call(functools.partial(pack_body, slots, first, experts), grid=...  9.79 us
  transfers between devices with their start and end apart: 7, of which 4 were waited for; matrix products, arithmetic and copies ran while one was open for 1% of the time, Pallas kernels for 25%

profile of v2, /device:TPU:12, one launch (start us, length us, event | category | flops | bytes accessed | tf_op | source)
XLA Modules:
  0.0 272.7 jit_solution(15962398711996205483)
XLA Ops:
  0.0 5.5 %pack.3 = bf16[1536,1792]{1,0:T(8,128)(2,1)} custom-call(s32[8,64]{1,0:T(8,128)} %bitcast.13, bf16[64,7168]{1,0:T(8,128)(2,1)} %tokens_ref.3), custom_call_target="tpu_custom_call" | custom-call | flops 1409286144 | bytes 5505024 | tf_op jit(solution)/shard_map/pack/pallas_call | solution.py:84
  5.5 11.5 %all-to-all-start.2 = ((bf16[64,24,1792]{2,1,0:T(8,128)(2,1)}), bf16[64,24,1792]{2,1,0:T(8,128)(2,1)}, u32[]{:S(2)}, u32[]{:S(2)}) async-start(bf16[64,24,1792]{2,1,0:T(8,128)(2,1)} %bitcast.9), calls=%async_computation.2 | async-start | bytes 11010048 | tf_op jit(solution)/shard_map/all_to_all | solution.py:270
  17.1 0.1 collective-permute-start
  17.2 0.5 collective-permute-start.1
  17.6 0.1 collective-permute-start.2
  17.7 4.3 %pack.2 = bf16[1024,1792]{1,0:T(8,128)(2,1)} custom-call(s32[8,64]{1,0:T(8,128)} %bitcast.14, bf16[64,7168]{1,0:T(8,128)(2,1)} %tokens_ref.3), custom_call_target="tpu_custom_call" | custom-call | flops 939524096 | bytes 3670016 | tf_op jit(solution)/shard_map/pack/pallas_call | solution.py:84
  22.0 60.5 %all-to-all-done.2 = bf16[64,24,1792]{2,1,0:T(8,128)(2,1)} async-done(((bf16[64,24,1792]{2,1,0:T(8,128)(2,1)}), bf16[64,24,1792]{2,1,0:T(8,128)(2,1)}, u32[]{:S(2)}, u32[]{:S(2)}) %all-to-all-start.2) | async-done | bytes 5505056 | tf_op jit(solution)/shard_map/all_to_all | solution.py:270
  82.5 10.9 %all-to-all-start = ((bf16[64,16,1792]{2,1,0:T(8,128)(2,1)}), bf16[64,16,1792]{2,1,0:T(8,128)(2,1)}, u32[]{:S(2)}, u32[]{:S(2)}) async-start(bf16[64,16,1792]{2,1,0:T(8,128)(2,1)} %bitcast.11), calls=%async_computation | async-start | bytes 7340032 | tf_op jit(solution)/shard_map/all_to_all | solution.py:270
  93.4 0.0 collective-permute-done.gb
  93.4 0.0 collective-permute-done.1.ub
  93.4 0.0 collective-permute-done.2.db
  93.4 31.8 %experts.3 = bf16[1536,1792]{1,0:T(8,128)(2,1)} custom-call(bf16[1536,1792]{1,0:T(8,128)(2,1)} %bitcast.6.rows_in, bf16[1,7168,512]{2,1,0:T(8,128)(2,1)} %ga.3, bf16[1,7168,512]{2,1,0:T(8,128)(2,1)} %collective-permute-done.gb, bf16[1,7168,512]{2,1,0:T(8,128)(2,1)} %ua.3, bf16[1,7168,512]{2,1,0:T(8,128)(2,1)} %collective-permute-done.1.ub, ...), custom_call_target="tpu_custom_call" | custom-call | flops 16911433728 | bytes 55050240 | tf_op jit(solution)/shard_map/experts/pallas_call | solution.py:172
  125.2 12.5 %all-to-all-done = bf16[64,16,1792]{2,1,0:T(8,128)(2,1)} async-done(((bf16[64,16,1792]{2,1,0:T(8,128)(2,1)}), bf16[64,16,1792]{2,1,0:T(8,128)(2,1)}, u32[]{:S(2)}, u32[]{:S(2)}) %all-to-all-start) | async-done | bytes 3670048 | tf_op jit(solution)/shard_map/all_to_all | solution.py:270
  137.7 9.5 %all-to-all-start.3 = ((bf16[64,24,1792]{2,1,0:T(8,128)(2,1)}), bf16[64,24,1792]{2,1,0:T(8,128)(2,1)}, u32[]{:S(2)}, u32[]{:S(2)}) async-start(bf16[64,24,1792]{2,1,0:T(8,128)(2,1)} %bitcast.12), calls=%async_computation.3 | async-start | bytes 11010048 | tf_op jit(solution)/shard_map/all_to_all | solution.py:270
  147.2 26.2 %experts.2 = bf16[1024,1792]{1,0:T(8,128)(2,1)} custom-call(bf16[1024,1792]{1,0:T(8,128)(2,1)} %bitcast.2.rows_in, bf16[1,7168,512]{2,1,0:T(8,128)(2,1)} %ga.3, bf16[1,7168,512]{2,1,0:T(8,128)(2,1)} %collective-permute-done.gb, bf16[1,7168,512]{2,1,0:T(8,128)(2,1)} %ua.3, bf16[1,7168,512]{2,1,0:T(8,128)(2,1)} %collective-permute-done.1.ub, ...), custom_call_target="tpu_custom_call" | custom-call | flops 11274289152 | bytes 51380224 | tf_op jit(solution)/shard_map/experts/pallas_call | solution.py:172
  173.4 0.0 copy-start
  173.4 0.0 copy-start.1
  173.4 39.3 %all-to-all-done.3 = bf16[64,24,1792]{2,1,0:T(8,128)(2,1)} async-done(((bf16[64,24,1792]{2,1,0:T(8,128)(2,1)}), bf16[64,24,1792]{2,1,0:T(8,128)(2,1)}, u32[]{:S(2)}, u32[]{:S(2)}) %all-to-all-start.3) | async-done | bytes 5505056 | tf_op jit(solution)/shard_map/all_to_all | solution.py:270
  212.8 10.6 %all-to-all-start.1 = ((bf16[64,16,1792]{2,1,0:T(8,128)(2,1)}), bf16[64,16,1792]{2,1,0:T(8,128)(2,1)}, u32[]{:S(2)}, u32[]{:S(2)}) async-start(bf16[64,16,1792]{2,1,0:T(8,128)(2,1)} %bitcast.10), calls=%async_computation.1 | async-start | bytes 7340032 | tf_op jit(solution)/shard_map/all_to_all | solution.py:270
  223.4 0.0 copy-done
  223.4 0.7 copy.9.refs_0_
  224.1 0.0 copy-done.1
  224.1 0.7 copy.10.refs_1_
  224.8 7.1 %mix.2.refs_3_ = f32[64,7168]{1,0:T(8,128)} custom-call(s32[64,8]{1,0:T(8,128)} %copy.9.refs_0_, f32[64,8]{1,0:T(8,128)} %copy.10.refs_1_, bf16[1536,1792]{1,0:T(8,128)(2,1)} %bitcast.8.refs_2_), custom_call_target="tpu_custom_call" | custom-call | flops 1409286144 | bytes 5505024 | tf_op jit(solution)/shard_map/mix/pallas_call | solution.py:247
  231.8 35.5 %all-to-all-done.1 = bf16[64,16,1792]{2,1,0:T(8,128)(2,1)} async-done(((bf16[64,16,1792]{2,1,0:T(8,128)(2,1)}), bf16[64,16,1792]{2,1,0:T(8,128)(2,1)}, u32[]{:S(2)}, u32[]{:S(2)}) %all-to-all-start.1) | async-done | bytes 3670048 | tf_op jit(solution)/shard_map/all_to_all | solution.py:270
  267.3 5.4 %mix.3 = bf16[64,7168]{1,0:T(8,128)(2,1)} custom-call(s32[64,8]{1,0:T(8,128)} %copy.9.refs_0_, f32[64,8]{1,0:T(8,128)} %copy.10.refs_1_, bf16[1024,1792]{1,0:T(8,128)(2,1)} %bitcast.4.refs_2_, f32[64,7168]{1,0:T(8,128)} %mix.2.refs_3_), custom_call_target="tpu_custom_call" | custom-call | flops 939524096 | bytes 3670016 | tf_op jit(solution)/shard_map/mix/pallas_call | solution.py:247
Async XLA Ops:
  5.5 77.0 %all-to-all-start.2 = ((bf16[64,24,1792]{2,1,0:T(8,128)(2,1)}), bf16[64,24,1792]{2,1,0:T(8,128)(2,1)}, u32[]{:S(2)}, u32[]{:S(2)}) async-start(bf16[64,24,1792]{2,1,0:T(8,128)(2,1)} %bitcast.9), calls=%async_computation.2 | async-start | bytes 11010048 | tf_op jit(solution)/shard_map/all_to_all | solution.py:270
  17.1 76.3 %collective-permute-start = (bf16[1,7168,512]{2,1,0:T(8,128)(2,1)}, bf16[1,7168,512]{2,1,0:T(8,128)(2,1)}, u32[]{:S(2)}, u32[]{:S(2)}) collective-permute-start(bf16[1,7168,512]{2,1,0:T(8,128)(2,1)} %ga.3), channel_id=1, source_target_pairs={{0,1},{1,0},{2,3},{3,2},{4,5},{5,4},{6,7},{7,6},{8,9},{9,8},{10,11... | collective-permute-start | bytes 22020104 | tf_op jit(solution)/shard_map/ppermute | solution.py:276
  17.2 76.2 %collective-permute-start.1 = (bf16[1,7168,512]{2,1,0:T(8,128)(2,1)}, bf16[1,7168,512]{2,1,0:T(8,128)(2,1)}, u32[]{:S(2)}, u32[]{:S(2)}) collective-permute-start(bf16[1,7168,512]{2,1,0:T(8,128)(2,1)} %ua.3), channel_id=1, source_target_pairs={{0,1},{1,0},{2,3},{3,2},{4,5},{5,4},{6,7},{7,6},{8,9},{9,8},{10,11... | collective-permute-start | bytes 22020104 | tf_op jit(solution)/shard_map/ppermute | solution.py:276
  17.6 75.8 %collective-permute-start.2 = (bf16[1,512,7168]{2,1,0:T(8,128)(2,1)}, bf16[1,512,7168]{2,1,0:T(8,128)(2,1)}, u32[]{:S(2)}, u32[]{:S(2)}) collective-permute-start(bf16[1,512,7168]{2,1,0:T(8,128)(2,1)} %da.3), channel_id=1, source_target_pairs={{0,1},{1,0},{2,3},{3,2},{4,5},{5,4},{6,7},{7,6},{8,9},{9,8},{10,11... | collective-permute-start | bytes 22020104 | tf_op jit(solution)/shard_map/ppermute | solution.py:276
  82.5 55.2 %all-to-all-start = ((bf16[64,16,1792]{2,1,0:T(8,128)(2,1)}), bf16[64,16,1792]{2,1,0:T(8,128)(2,1)}, u32[]{:S(2)}, u32[]{:S(2)}) async-start(bf16[64,16,1792]{2,1,0:T(8,128)(2,1)} %bitcast.11), calls=%async_computation | async-start | bytes 7340032 | tf_op jit(solution)/shard_map/all_to_all | solution.py:270
  137.7 75.1 %all-to-all-start.3 = ((bf16[64,24,1792]{2,1,0:T(8,128)(2,1)}), bf16[64,24,1792]{2,1,0:T(8,128)(2,1)}, u32[]{:S(2)}, u32[]{:S(2)}) async-start(bf16[64,24,1792]{2,1,0:T(8,128)(2,1)} %bitcast.12), calls=%async_computation.3 | async-start | bytes 11010048 | tf_op jit(solution)/shard_map/all_to_all | solution.py:270
  173.4 50.0 %copy-start = (s32[64,8]{0,1:T(8,128)S(1)}, s32[64,8]{0,1:T(8,128)}, u32[]{:S(2)}) copy-start(s32[64,8]{0,1:T(8,128)} %param.7) | copy-start | bytes 6148
  173.4 50.7 %copy-start.1 = (f32[64,8]{0,1:T(8,128)S(1)}, f32[64,8]{0,1:T(8,128)}, u32[]{:S(2)}) copy-start(f32[64,8]{0,1:T(8,128)} %param.8) | copy-start | bytes 6148
  212.8 54.5 %all-to-all-start.1 = ((bf16[64,16,1792]{2,1,0:T(8,128)(2,1)}), bf16[64,16,1792]{2,1,0:T(8,128)(2,1)}, u32[]{:S(2)}, u32[]{:S(2)}) async-start(bf16[64,16,1792]{2,1,0:T(8,128)(2,1)} %bitcast.10), calls=%async_computation.1 | async-start | bytes 7340032 | tf_op jit(solution)/shard_map/all_to_all | solution.py:270

commit v3 on v2

--- a/solution.py
+++ b/solution.py
@@ -15,6 +15,7 @@
 SLOTS = (6, 4)
 BLOCK = 512
 VMEM = 60 << 20
+SMALL = 20 << 20
 F32 = jnp.float32
 BF16 = jnp.bfloat16
 
@@ -46,53 +47,50 @@
     return jnp.dot(a, b, preferred_element_type=F32)
 
 
-def pack_body(slots, first, experts, routes_ref, tokens_ref, out_ref, codes_ref, tok_ref):
-    rows, width = out_ref.shape
-    toks = tokens_ref.shape[0]
-    step = pl.program_id(0)
-
-    @pl.when(step == 0)
-    def _():
-        names = iota((experts, toks), 0)
-        hits = jnp.zeros((experts, toks), F32)
-        for k in range(routes_ref.shape[0]):
-            hits = hits + (routes_ref[k : k + 1, :] == names).astype(F32)
-        before = (iota((toks, toks), 0) < iota((toks, toks), 1)).astype(F32).astype(BF16)
-        earlier = dot(hits.astype(BF16), before)
-        codes = (hits * (earlier + 1.0)).astype(BF16)
-        wide = (toks, PARTS * toks)
-        spread = ((iota(wide, 1) & (toks - 1)) == iota(wide, 0)).astype(F32).astype(BF16)
-        codes_ref[...] = dot(codes, spread).astype(BF16)
-        for s in range(PARTS):
-            tok_ref[s * toks : (s + 1) * toks, :] = tokens_ref[:, s * width : (s + 1) * width]
-
-    row = step * rows + iota((rows, 1), 0)
-    expert, rank = expert_and_rank(lax.div(row, PARTS), slots, first)
-    named = (iota((rows, experts), 1) == expert).astype(F32).astype(BF16)
-    found = dot(named, codes_ref[...])
-    wide = (rows, PARTS * toks)
-    want = jnp.where(lax.div(iota(wide, 1), toks) == lax.rem(row, PARTS), (rank + 1).astype(F32), -1.0)
-    picks = jnp.where(found == want, 1.0, 0.0).astype(BF16)
-    out_ref[...] = dot(picks, tok_ref[...]).astype(BF16)
+def pack_body(slots, first, routes_ref, tokens_ref, out_ref, tok_ref, ready, sems):
+    toks = routes_ref.shape[1]
+    total, width = ready.shape
+    experts = total // (slots * PARTS)
+    for s in range(PARTS):
+        tok_ref[s * toks : (s + 1) * toks, :] = tokens_ref[:, s * width : (s + 1) * width]
+    names = iota((experts, toks), 0)
+    hits = jnp.zeros((experts, toks), F32)
+    for k in range(routes_ref.shape[0]):
+        hits = hits + (routes_ref[k : k + 1, :] == names).astype(F32)
+    before = (iota((toks, toks), 0) < iota((toks, toks), 1)).astype(F32).astype(BF16)
+    earlier = dot(hits.astype(BF16), before)
+    codes = (hits * (earlier + 1.0)).astype(BF16)
+    codes = jnp.concatenate([codes] * PARTS, axis=1)
+    copies = []
+    for n in range(total // BLOCK):
+        at = slice(n * BLOCK, (n + 1) * BLOCK)
+        row = n * BLOCK + iota((BLOCK, 1), 0)
+        expert, rank = expert_and_rank(lax.div(row, PARTS), slots, first)
+        named = (iota((BLOCK, experts), 1) == expert).astype(F32).astype(BF16)
+        found = dot(named, codes)
+        wide = (BLOCK, PARTS * toks)
+        want = jnp.where(lax.div(iota(wide, 1), toks) == lax.rem(row, PARTS), (rank + 1).astype(F32), -1.0)
+        picks = jnp.where(found == want, 1.0, 0.0).astype(BF16)
+        ready[at, :] = dot(picks, tok_ref[...]).astype(BF16)
+        copies.append(pltpu.make_async_copy(ready.at[at, :], out_ref.at[at, :], sems.at[n]))
+        copies[-1].start()
+    for copy in copies:
+        copy.wait()
 
 
 def pack(routes_t, tokens, slots, first, experts):
     toks, width = tokens.shape
     part = width // PARTS
     rows = experts * slots * PARTS
-    block = BLOCK
     return pl.pallas_call(
-        functools.partial(pack_body, slots, first, experts),
-        grid=(rows // block,),
+        functools.partial(pack_body, slots, first),
         out_shape=jax.ShapeDtypeStruct((rows, part), BF16),
-        in_specs=[
-            pl.BlockSpec(routes_t.shape, lambda i: (0, 0)),
-            pl.BlockSpec(tokens.shape, lambda i: (0, 0)),
-        ],
-        out_specs=pl.BlockSpec((block, part), lambda i: (i, 0)),
+        in_specs=[pl.BlockSpec(memory_space=pltpu.VMEM)] * 2,
+        out_specs=pl.BlockSpec(memory_space=pl.ANY),
         scratch_shapes=[
-            pltpu.VMEM((experts, PARTS * toks), BF16),
             pltpu.VMEM((PARTS * toks, part), BF16),
+            pltpu.VMEM((rows, part), BF16),
+            pltpu.SemaphoreType.DMA((rows // BLOCK,)),
         ],
         compiler_params=pltpu.CompilerParams(vmem_limit_bytes=VMEM),
         cost_estimate=pl.CostEstimate(
@@ -198,70 +196,92 @@
     )(rows_in, gate, gate_other, up, up_other, down, down_other)
 
 
-def mix_body(slots, first, experts, blocks, with_sum, *refs):
-    if with_sum:
-        routes_ref, gates_ref, rows_ref, sum_ref, out_ref, parts = refs
-    else:
-        routes_ref, gates_ref, rows_ref, out_ref, parts = refs
-    step = pl.program_id(0)
-    part = rows_ref.shape[1]
+def plan_body(chunks, experts, routes_ref, gates_ref, *outs):
     toks = routes_ref.shape[0]
-    split(step, rows_ref, parts)
-
-    @pl.when(step == blocks - 1)
-    def _():
-        rows = parts.shape[1]
-        names = iota((toks, experts), 1)
-        hits = jnp.zeros((toks, experts), F32)
-        weight = jnp.zeros((toks, experts), F32)
-        for k in range(routes_ref.shape[1]):
-            hit = (routes_ref[:, k : k + 1] == names).astype(F32)
-            hits = hits + hit
-            weight = weight + hit * gates_ref[:, k : k + 1]
-        before = (iota((toks, toks), 1) < iota((toks, toks), 0)).astype(F32).astype(BF16)
-        codes = (hits * (dot(before, hits.astype(BF16)) + 1.0)).astype(BF16)
-        high = weight.astype(BF16)
-        low = (weight - high.astype(F32)).astype(BF16)
+    names = iota((toks, experts), 1)
+    hits = jnp.zeros((toks, experts), F32)
+    weight = jnp.zeros((toks, experts), F32)
+    for k in range(routes_ref.shape[1]):
+        hit = (routes_ref[:, k : k + 1] == names).astype(F32)
+        hits = hits + hit
+        weight = weight + hit * gates_ref[:, k : k + 1]
+    before = (iota((toks, toks), 1) < iota((toks, toks), 0)).astype(F32).astype(BF16)
+    codes = (hits * (dot(before, hits.astype(BF16)) + 1.0)).astype(BF16)
+    high = weight.astype(BF16)
+    low = (weight - high.astype(F32)).astype(BF16)
+    for (slots, first), out_ref in zip(chunks, outs):
+        rows = out_ref.shape[1]
         expert, rank = expert_and_rank(iota((1, rows), 1), slots, first)
         spread = (iota((experts, rows), 0) == expert).astype(F32).astype(BF16)
         here = dot(codes, spread) == (rank + 1).astype(F32)
-        high = jnp.where(here, dot(high, spread), 0.0).astype(BF16)
-        low = jnp.where(here, dot(low, spread), 0.0).astype(BF16)
-        both = jnp.concatenate([high, low], axis=0)
-        for s in range(PARTS):
-            value = dot(both, parts[s])
-            value = value[:toks] + value[toks:]
-            at = slice(s * part, (s + 1) * part)
-            if with_sum:
-                value = value + sum_ref[:, at]
-            out_ref[:, at] = value.astype(out_ref.dtype)
-
-
-def mix(routes, gates, rows_in, so_far, slots, first, experts, dtype):
+        for h, half in enumerate((high, low)):
+            placed = jnp.where(here, dot(half, spread), 0.0)
+            out_ref[h * toks : (h + 1) * toks, :] = placed.astype(BF16)
+
+
+def plan(routes, gates, chunks, experts):
+    toks = routes.shape[0]
+    sizes = [experts * n for n, _ in chunks]
+    return pl.pallas_call(
+        functools.partial(plan_body, chunks, experts),
+        out_shape=[jax.ShapeDtypeStruct((2 * toks, size), BF16) for size in sizes],
+        compiler_params=pltpu.CompilerParams(vmem_limit_bytes=SMALL),
+        cost_estimate=pl.CostEstimate(
+            flops=6 * toks * experts * sum(sizes), bytes_accessed=4 * toks * sum(sizes), transcendentals=0
+        ),
+        name="plan",
+    )(routes, gates)
+
+
+def mix_body(weights_ref, rows_hbm, *refs):
+    sum_ref, out_hbm, rows_ref, parts, result, in_sems, out_sems = refs if len(refs) == 7 else (None, *refs)
+    total, part = rows_ref.shape
+    toks = result.shape[0]
+    arrivals = []
+    for n in range(total // BLOCK):
+        at = slice(n * BLOCK, (n + 1) * BLOCK)
+        arrivals.append(pltpu.make_async_copy(rows_hbm.at[at, :], rows_ref.at[at, :], in_sems.at[n]))
+        arrivals[-1].start()
+    for n, arrival in enumerate(arrivals):
+        arrival.wait()
+        split(n, rows_ref.at[n * BLOCK : (n + 1) * BLOCK, :], parts)
+    departures = []
+    for s in range(PARTS):
+        value = dot(weights_ref[...], parts[s])
+        value = value[:toks] + value[toks:]
+        at = slice(s * part, (s + 1) * part)
+        if sum_ref is not None:
+            value = value + sum_ref[:, at]
+        result[:, at] = value.astype(result.dtype)
+        departures.append(pltpu.make_async_copy(result.at[:, at], out_hbm.at[:, at], out_sems.at[s]))
+        departures[-1].start()
+    for departure in departures:
+        departure.wait()
+
+
+def mix(weights, rows_in, so_far, dtype):
     total, part = rows_in.shape
-    toks = routes.shape[0]
-    block = BLOCK
-    blocks = total // block
-    whole = lambda i: (0, 0)
+    toks = weights.shape[0] // 2
+    here = pl.BlockSpec(memory_space=pltpu.VMEM)
     extra = () if so_far is None else (so_far,)
     return pl.pallas_call(
-        functools.partial(mix_body, slots, first, experts, blocks, bool(extra)),
-        grid=(blocks,),
+        mix_body,
         out_shape=jax.ShapeDtypeStruct((toks, part * PARTS), dtype),
-        in_specs=[
-            pl.BlockSpec(routes.shape, whole),
-            pl.BlockSpec(gates.shape, whole),
-            pl.BlockSpec((block, part), lambda i: (i, 0)),
-        ]
-        + [pl.BlockSpec(x.shape, whole) for x in extra],
-        out_specs=pl.BlockSpec((toks, part * PARTS), whole),
-        scratch_shapes=[pltpu.VMEM((PARTS, total // PARTS, part), BF16)],
-        compiler_params=pltpu.CompilerParams(vmem_limit_bytes=VMEM),
+        in_specs=[here, pl.BlockSpec(memory_space=pl.ANY)] + [here for _ in extra],
+        out_specs=pl.BlockSpec(memory_space=pl.ANY),
+        scratch_shapes=[
+            pltpu.VMEM((total, part), BF16),
+            pltpu.VMEM((PARTS, total // PARTS, part), BF16),
+            pltpu.VMEM((toks, part * PARTS), dtype),
+            pltpu.SemaphoreType.DMA((total // BLOCK,)),
+            pltpu.SemaphoreType.DMA((PARTS,)),
+        ],
+        compiler_params=pltpu.CompilerParams(vmem_limit_bytes=SMALL),
         cost_estimate=pl.CostEstimate(
             flops=2 * total * TILE * part, bytes_accessed=2 * total * part, transcendentals=0
         ),
         name="mix",
-    )(routes, gates, rows_in, *extra)
+    )(weights, rows_in, *extra)
 
 
 def exchange(rows, experts):
@@ -284,9 +304,8 @@
     ]
     back = [exchange(d, experts) for d in done]
     mixed = None
-    for at, (n, f) in enumerate(zip(SLOTS, firsts)):
-        dtype = BF16 if at == len(SLOTS) - 1 else F32
-        mixed = mix(routes, gates, back[at], mixed, n, f, experts, dtype)
+    for at, weights in enumerate(plan(routes, gates, tuple(zip(SLOTS, firsts)), experts)):
+        mixed = mix(weights, back[at], mixed, BF16 if at == len(SLOTS) - 1 else F32)
     return mixed
 
 

time: 276 us -> 274 us (level)
  Pallas kernels: 80.2 us -> 76.6 us
    pallas_call x4 -> x5, Pallas kernels: 22.2 us -> 18.5 us  [the longest x2 9.29 us: mix(): pl.pallas_call(mix_body, out_shape=jax.ShapeDtypeStruct((toks, part * PAR...]
  transfers between devices with their start and end apart: 7 -> 7, of which waited for: 4 -> 4; matrix products, arithmetic and copies ran while one was open for 1% -> 0% of each run, Pallas kernels for 25% -> 25%
where the time goes in v3:
time: 274 us; the launch traced here: 271 us
  waiting for transfers between devices  150 us (55%)
  Pallas kernels  76.6 us (28%)
  starting transfers between devices  43.2 us (16%)
    all_to_all x4, waiting for transfers between devices, exchange(): lax.all_to_all(rows, CHIPS, split_axis=0, concat_axis=0, tiled=True)  150 us
    pallas_call x2, Pallas kernels, ffn(): pl.pallas_call(functools.partial(ffn_body, blocks), grid=(2 * blocks + 2...  58.1 us
    all_to_all x4, starting transfers between devices, exchange(): lax.all_to_all(rows, CHIPS, split_axis=0, concat_axis=0, tiled=True)  42.5 us
    pallas_call x2, Pallas kernels, mix(): pl.pallas_call(mix_body, out_shape=jax.ShapeDtypeStruct((toks, part * PAR...  9.29 us
    pallas_call x2, Pallas kernels, pack(): pl.pallas_call(functools.partial(pack_body, slots, first), out_shape=jax....  8.72 us
  transfers between devices with their start and end apart: 7, of which 4 were waited for; matrix products, arithmetic and copies ran while one was open for 0% of the time, Pallas kernels for 25%

profile of v3, /device:TPU:12, one launch (start us, length us, event | category | flops | bytes accessed | tf_op | source)
XLA Modules:
  0.0 270.7 jit_solution(12425901529644752488)
XLA Ops:
  0.0 4.7 %pack.3 = bf16[1536,1792]{1,0:T(8,128)(2,1)} custom-call(s32[8,64]{1,0:T(8,128)} %bitcast.13, bf16[64,7168]{1,0:T(8,128)(2,1)} %tokens_ref.3), custom_call_target="tpu_custom_call" | custom-call | flops 1409286144 | bytes 5505024 | tf_op jit(solution)/shard_map/pack/pallas_call | solution.py:85
  4.7 11.5 %all-to-all-start.2 = ((bf16[64,24,1792]{2,1,0:T(8,128)(2,1)}), bf16[64,24,1792]{2,1,0:T(8,128)(2,1)}, u32[]{:S(2)}, u32[]{:S(2)}) async-start(bf16[64,24,1792]{2,1,0:T(8,128)(2,1)} %bitcast.9), calls=%async_computation.2 | async-start | bytes 11010048 | tf_op jit(solution)/shard_map/all_to_all | solution.py:290
  16.2 0.1 collective-permute-start
  16.3 0.5 collective-permute-start.1
  16.8 0.1 collective-permute-start.2
  16.9 4.0 %pack.2 = bf16[1024,1792]{1,0:T(8,128)(2,1)} custom-call(s32[8,64]{1,0:T(8,128)} %bitcast.14, bf16[64,7168]{1,0:T(8,128)(2,1)} %tokens_ref.3), custom_call_target="tpu_custom_call" | custom-call | flops 939524096 | bytes 3670016 | tf_op jit(solution)/shard_map/pack/pallas_call | solution.py:85
  21.0 60.7 %all-to-all-done.2 = bf16[64,24,1792]{2,1,0:T(8,128)(2,1)} async-done(((bf16[64,24,1792]{2,1,0:T(8,128)(2,1)}), bf16[64,24,1792]{2,1,0:T(8,128)(2,1)}, u32[]{:S(2)}, u32[]{:S(2)}) %all-to-all-start.2) | async-done | bytes 5505056 | tf_op jit(solution)/shard_map/all_to_all | solution.py:290
  81.7 10.9 %all-to-all-start = ((bf16[64,16,1792]{2,1,0:T(8,128)(2,1)}), bf16[64,16,1792]{2,1,0:T(8,128)(2,1)}, u32[]{:S(2)}, u32[]{:S(2)}) async-start(bf16[64,16,1792]{2,1,0:T(8,128)(2,1)} %bitcast.11), calls=%async_computation | async-start | bytes 7340032 | tf_op jit(solution)/shard_map/all_to_all | solution.py:290
  92.6 0.0 collective-permute-done.gb
  92.6 0.0 collective-permute-done.1.ub
  92.6 0.0 collective-permute-done.2.db
  92.6 31.8 %experts.3 = bf16[1536,1792]{1,0:T(8,128)(2,1)} custom-call(bf16[1536,1792]{1,0:T(8,128)(2,1)} %bitcast.6.rows_in, bf16[1,7168,512]{2,1,0:T(8,128)(2,1)} %ga.3, bf16[1,7168,512]{2,1,0:T(8,128)(2,1)} %collective-permute-done.gb, bf16[1,7168,512]{2,1,0:T(8,128)(2,1)} %ua.3, bf16[1,7168,512]{2,1,0:T(8,128)(2,1)} %collective-permute-done.1.ub, ...), custom_call_target="tpu_custom_call" | custom-call | flops 16911433728 | bytes 55050240 | tf_op jit(solution)/shard_map/experts/pallas_call | solution.py:170
  124.4 12.4 %all-to-all-done = bf16[64,16,1792]{2,1,0:T(8,128)(2,1)} async-done(((bf16[64,16,1792]{2,1,0:T(8,128)(2,1)}), bf16[64,16,1792]{2,1,0:T(8,128)(2,1)}, u32[]{:S(2)}, u32[]{:S(2)}) %all-to-all-start) | async-done | bytes 3670048 | tf_op jit(solution)/shard_map/all_to_all | solution.py:290
  136.9 9.5 %all-to-all-start.3 = ((bf16[64,24,1792]{2,1,0:T(8,128)(2,1)}), bf16[64,24,1792]{2,1,0:T(8,128)(2,1)}, u32[]{:S(2)}, u32[]{:S(2)}) async-start(bf16[64,24,1792]{2,1,0:T(8,128)(2,1)} %bitcast.12), calls=%async_computation.3 | async-start | bytes 11010048 | tf_op jit(solution)/shard_map/all_to_all | solution.py:290
  146.4 26.3 %experts.2 = bf16[1024,1792]{1,0:T(8,128)(2,1)} custom-call(bf16[1024,1792]{1,0:T(8,128)(2,1)} %bitcast.2.rows_in, bf16[1,7168,512]{2,1,0:T(8,128)(2,1)} %ga.3, bf16[1,7168,512]{2,1,0:T(8,128)(2,1)} %collective-permute-done.gb, bf16[1,7168,512]{2,1,0:T(8,128)(2,1)} %ua.3, bf16[1,7168,512]{2,1,0:T(8,128)(2,1)} %collective-permute-done.1.ub, ...), custom_call_target="tpu_custom_call" | custom-call | flops 11274289152 | bytes 51380224 | tf_op jit(solution)/shard_map/experts/pallas_call | solution.py:170
  172.6 0.0 copy-start
  172.6 0.0 copy-start.1
  172.6 39.3 %all-to-all-done.3 = bf16[64,24,1792]{2,1,0:T(8,128)(2,1)} async-done(((bf16[64,24,1792]{2,1,0:T(8,128)(2,1)}), bf16[64,24,1792]{2,1,0:T(8,128)(2,1)}, u32[]{:S(2)}, u32[]{:S(2)}) %all-to-all-start.3) | async-done | bytes 5505056 | tf_op jit(solution)/shard_map/all_to_all | solution.py:290
  211.9 10.6 %all-to-all-start.1 = ((bf16[64,16,1792]{2,1,0:T(8,128)(2,1)}), bf16[64,16,1792]{2,1,0:T(8,128)(2,1)}, u32[]{:S(2)}, u32[]{:S(2)}) async-start(bf16[64,16,1792]{2,1,0:T(8,128)(2,1)} %bitcast.10), calls=%async_computation.1 | async-start | bytes 7340032 | tf_op jit(solution)/shard_map/all_to_all | solution.py:290
  222.5 0.0 copy-done
  222.6 0.1 copy.7.routes_ref
  222.6 0.0 copy-done.1
  222.6 0.1 copy.8.gates_ref
  222.7 0.5 plan.1
  223.2 5.3 %mix.2.refs_0_ = f32[64,7168]{1,0:T(8,128)S(1)} custom-call(bf16[128,384]{1,0:T(8,128)(2,1)S(1)} %get-tuple-element.8.weights_ref, bf16[1536,1792]{1,0:T(8,128)(2,1)} %bitcast.8.rows_hbm), custom_call_target="tpu_custom_call" | custom-call | flops 1409286144 | bytes 5505024 | tf_op jit(solution)/shard_map/mix/pallas_call | solution.py:267
  228.5 38.0 %all-to-all-done.1 = bf16[64,16,1792]{2,1,0:T(8,128)(2,1)} async-done(((bf16[64,16,1792]{2,1,0:T(8,128)(2,1)}), bf16[64,16,1792]{2,1,0:T(8,128)(2,1)}, u32[]{:S(2)}, u32[]{:S(2)}) %all-to-all-start.1) | async-done | bytes 3670048 | tf_op jit(solution)/shard_map/all_to_all | solution.py:290
  266.5 4.0 %mix.3 = bf16[64,7168]{1,0:T(8,128)(2,1)} custom-call(bf16[128,256]{1,0:T(8,128)(2,1)S(1)} %get-tuple-element.7.weights_ref, bf16[1024,1792]{1,0:T(8,128)(2,1)} %bitcast.4.rows_hbm, f32[64,7168]{1,0:T(8,128)S(1)} %mix.2.refs_0_), custom_call_target="tpu_custom_call" | custom-call | flops 939524096 | bytes 3670016 | tf_op jit(solution)/shard_map/mix/pallas_call | solution.py:267
Async XLA Ops:
  4.7 77.0 %all-to-all-start.2 = ((bf16[64,24,1792]{2,1,0:T(8,128)(2,1)}), bf16[64,24,1792]{2,1,0:T(8,128)(2,1)}, u32[]{:S(2)}, u32[]{:S(2)}) async-start(bf16[64,24,1792]{2,1,0:T(8,128)(2,1)} %bitcast.9), calls=%async_computation.2 | async-start | bytes 11010048 | tf_op jit(solution)/shard_map/all_to_all | solution.py:290
  16.2 76.3 %collective-permute-start = (bf16[1,7168,512]{2,1,0:T(8,128)(2,1)}, bf16[1,7168,512]{2,1,0:T(8,128)(2,1)}, u32[]{:S(2)}, u32[]{:S(2)}) collective-permute-start(bf16[1,7168,512]{2,1,0:T(8,128)(2,1)} %ga.3), channel_id=1, source_target_pairs={{0,1},{1,0},{2,3},{3,2},{4,5},{5,4},{6,7},{7,6},{8,9},{9,8},{10,11... | collective-permute-start | bytes 22020104 | tf_op jit(solution)/shard_map/ppermute | solution.py:296
  16.3 76.2 %collective-permute-start.1 = (bf16[1,7168,512]{2,1,0:T(8,128)(2,1)}, bf16[1,7168,512]{2,1,0:T(8,128)(2,1)}, u32[]{:S(2)}, u32[]{:S(2)}) collective-permute-start(bf16[1,7168,512]{2,1,0:T(8,128)(2,1)} %ua.3), channel_id=1, source_target_pairs={{0,1},{1,0},{2,3},{3,2},{4,5},{5,4},{6,7},{7,6},{8,9},{9,8},{10,11... | collective-permute-start | bytes 22020104 | tf_op jit(solution)/shard_map/ppermute | solution.py:296
  16.8 75.8 %collective-permute-start.2 = (bf16[1,512,7168]{2,1,0:T(8,128)(2,1)}, bf16[1,512,7168]{2,1,0:T(8,128)(2,1)}, u32[]{:S(2)}, u32[]{:S(2)}) collective-permute-start(bf16[1,512,7168]{2,1,0:T(8,128)(2,1)} %da.3), channel_id=1, source_target_pairs={{0,1},{1,0},{2,3},{3,2},{4,5},{5,4},{6,7},{7,6},{8,9},{9,8},{10,11... | collective-permute-start | bytes 22020104 | tf_op jit(solution)/shard_map/ppermute | solution.py:296
  81.7 55.2 %all-to-all-start = ((bf16[64,16,1792]{2,1,0:T(8,128)(2,1)}), bf16[64,16,1792]{2,1,0:T(8,128)(2,1)}, u32[]{:S(2)}, u32[]{:S(2)}) async-start(bf16[64,16,1792]{2,1,0:T(8,128)(2,1)} %bitcast.11), calls=%async_computation | async-start | bytes 7340032 | tf_op jit(solution)/shard_map/all_to_all | solution.py:290
  136.9 75.1 %all-to-all-start.3 = ((bf16[64,24,1792]{2,1,0:T(8,128)(2,1)}), bf16[64,24,1792]{2,1,0:T(8,128)(2,1)}, u32[]{:S(2)}, u32[]{:S(2)}) async-start(bf16[64,24,1792]{2,1,0:T(8,128)(2,1)} %bitcast.12), calls=%async_computation.3 | async-start | bytes 11010048 | tf_op jit(solution)/shard_map/all_to_all | solution.py:290
  172.6 49.9 %copy-start = (s32[64,8]{0,1:T(8,128)S(1)}, s32[64,8]{0,1:T(8,128)}, u32[]{:S(2)}) copy-start(s32[64,8]{0,1:T(8,128)} %param.7) | copy-start | bytes 6148
  172.6 50.0 %copy-start.1 = (f32[64,8]{0,1:T(8,128)S(1)}, f32[64,8]{0,1:T(8,128)}, u32[]{:S(2)}) copy-start(f32[64,8]{0,1:T(8,128)} %param.8) | copy-start | bytes 6148
  211.9 54.5 %all-to-all-start.1 = ((bf16[64,16,1792]{2,1,0:T(8,128)(2,1)}), bf16[64,16,1792]{2,1,0:T(8,128)(2,1)}, u32[]{:S(2)}, u32[]{:S(2)}) async-start(bf16[64,16,1792]{2,1,0:T(8,128)(2,1)} %bitcast.10), calls=%async_computation.1 | async-start | bytes 7340032 | tf_op jit(solution)/shard_map/all_to_all | solution.py:290

commit v4 on v3

--- a/solution.py
+++ b/solution.py
@@ -12,7 +12,7 @@
 PARTS = 4
 ROWS = 64
 TILE = ROWS * PARTS
-SLOTS = (6, 4)
+SLOTS = (4, 6)
 BLOCK = 512
 VMEM = 60 << 20
 SMALL = 20 << 20

time: 274 us -> 274 us (level)
  no operation moved by 1% of the time
where the time goes in v4:
time: 274 us; the launch traced here: 270 us
  waiting for transfers between devices  152 us (55%)
  Pallas kernels  76.3 us (28%)
  starting transfers between devices  41.1 us (15%)
    all_to_all x4, waiting for transfers between devices, exchange(): lax.all_to_all(rows, CHIPS, split_axis=0, concat_axis=0, tiled=True)  152 us
    pallas_call x2, Pallas kernels, ffn(): pl.pallas_call(functools.partial(ffn_body, blocks), grid=(2 * blocks + 2...  58 us
    all_to_all x4, starting transfers between devices, exchange(): lax.all_to_all(rows, CHIPS, split_axis=0, concat_axis=0, tiled=True)  40.4 us
    pallas_call x2, Pallas kernels, mix(): pl.pallas_call(mix_body, out_shape=jax.ShapeDtypeStruct((toks, part * PAR...  9.21 us
    pallas_call x2, Pallas kernels, pack(): pl.pallas_call(functools.partial(pack_body, slots, first), out_shape=jax....  8.59 us
  transfers between devices with their start and end apart: 7, of which 4 were waited for; matrix products, arithmetic and copies ran while one was open for 0% of the time, Pallas kernels for 25%

profile of v4, /device:TPU:12, one launch (start us, length us, event | category | flops | bytes accessed | tf_op | source)
XLA Modules:
  0.0 269.9 jit_solution(4375081636462994701)
XLA Ops:
  0.0 4.0 %pack.3 = bf16[1024,1792]{1,0:T(8,128)(2,1)} custom-call(s32[8,64]{1,0:T(8,128)} %bitcast.13, bf16[64,7168]{1,0:T(8,128)(2,1)} %tokens_ref.3), custom_call_target="tpu_custom_call" | custom-call | flops 939524096 | bytes 3670016 | tf_op jit(solution)/shard_map/pack/pallas_call | solution.py:85
  4.0 11.5 %all-to-all-start.2 = ((bf16[64,16,1792]{2,1,0:T(8,128)(2,1)}), bf16[64,16,1792]{2,1,0:T(8,128)(2,1)}, u32[]{:S(2)}, u32[]{:S(2)}) async-start(bf16[64,16,1792]{2,1,0:T(8,128)(2,1)} %bitcast.11), calls=%async_computation.2 | async-start | bytes 7340032 | tf_op jit(solution)/shard_map/all_to_all | solution.py:290
  15.5 0.1 collective-permute-start
  15.6 0.5 collective-permute-start.1
  16.1 0.1 collective-permute-start.2
  16.2 4.6 %pack.2 = bf16[1536,1792]{1,0:T(8,128)(2,1)} custom-call(s32[8,64]{1,0:T(8,128)} %bitcast.14, bf16[64,7168]{1,0:T(8,128)(2,1)} %tokens_ref.3), custom_call_target="tpu_custom_call" | custom-call | flops 1409286144 | bytes 5505024 | tf_op jit(solution)/shard_map/pack/pallas_call | solution.py:85
  20.8 39.2 %all-to-all-done.2 = bf16[64,16,1792]{2,1,0:T(8,128)(2,1)} async-done(((bf16[64,16,1792]{2,1,0:T(8,128)(2,1)}), bf16[64,16,1792]{2,1,0:T(8,128)(2,1)}, u32[]{:S(2)}, u32[]{:S(2)}) %all-to-all-start.2) | async-done | bytes 3670048 | tf_op jit(solution)/shard_map/all_to_all | solution.py:290
  60.0 9.5 %all-to-all-start = ((bf16[64,24,1792]{2,1,0:T(8,128)(2,1)}), bf16[64,24,1792]{2,1,0:T(8,128)(2,1)}, u32[]{:S(2)}, u32[]{:S(2)}) async-start(bf16[64,24,1792]{2,1,0:T(8,128)(2,1)} %bitcast.9), calls=%async_computation | async-start | bytes 11010048 | tf_op jit(solution)/shard_map/all_to_all | solution.py:290
  69.5 0.0 collective-permute-done.gb
  69.5 0.0 collective-permute-done.1.ub
  69.5 0.0 collective-permute-done.2.db
  69.5 26.2 %experts.3 = bf16[1024,1792]{1,0:T(8,128)(2,1)} custom-call(bf16[1024,1792]{1,0:T(8,128)(2,1)} %bitcast.6.rows_in, bf16[1,7168,512]{2,1,0:T(8,128)(2,1)} %ga.3, bf16[1,7168,512]{2,1,0:T(8,128)(2,1)} %collective-permute-done.gb, bf16[1,7168,512]{2,1,0:T(8,128)(2,1)} %ua.3, bf16[1,7168,512]{2,1,0:T(8,128)(2,1)} %collective-permute-done.1.ub, ...), custom_call_target="tpu_custom_call" | custom-call | flops 11274289152 | bytes 51380224 | tf_op jit(solution)/shard_map/experts/pallas_call | solution.py:170
  95.7 39.8 %all-to-all-done = bf16[64,24,1792]{2,1,0:T(8,128)(2,1)} async-done(((bf16[64,24,1792]{2,1,0:T(8,128)(2,1)}), bf16[64,24,1792]{2,1,0:T(8,128)(2,1)}, u32[]{:S(2)}, u32[]{:S(2)}) %all-to-all-start) | async-done | bytes 5505056 | tf_op jit(solution)/shard_map/all_to_all | solution.py:290
  135.5 10.8 %all-to-all-start.3 = ((bf16[64,16,1792]{2,1,0:T(8,128)(2,1)}), bf16[64,16,1792]{2,1,0:T(8,128)(2,1)}, u32[]{:S(2)}, u32[]{:S(2)}) async-start(bf16[64,16,1792]{2,1,0:T(8,128)(2,1)} %bitcast.10), calls=%async_computation.3 | async-start | bytes 7340032 | tf_op jit(solution)/shard_map/all_to_all | solution.py:290
  146.3 31.8 %experts.2 = bf16[1536,1792]{1,0:T(8,128)(2,1)} custom-call(bf16[1536,1792]{1,0:T(8,128)(2,1)} %bitcast.2.rows_in, bf16[1,7168,512]{2,1,0:T(8,128)(2,1)} %ga.3, bf16[1,7168,512]{2,1,0:T(8,128)(2,1)} %collective-permute-done.gb, bf16[1,7168,512]{2,1,0:T(8,128)(2,1)} %ua.3, bf16[1,7168,512]{2,1,0:T(8,128)(2,1)} %collective-permute-done.1.ub, ...), custom_call_target="tpu_custom_call" | custom-call | flops 16911433728 | bytes 55050240 | tf_op jit(solution)/shard_map/experts/pallas_call | solution.py:170
  178.1 12.0 %all-to-all-done.3 = bf16[64,16,1792]{2,1,0:T(8,128)(2,1)} async-done(((bf16[64,16,1792]{2,1,0:T(8,128)(2,1)}), bf16[64,16,1792]{2,1,0:T(8,128)(2,1)}, u32[]{:S(2)}, u32[]{:S(2)}) %all-to-all-start.3) | async-done | bytes 3670048 | tf_op jit(solution)/shard_map/all_to_all | solution.py:290
  190.1 0.0 copy-start
  190.1 0.0 copy-start.1
  190.1 8.7 %all-to-all-start.1 = ((bf16[64,24,1792]{2,1,0:T(8,128)(2,1)}), bf16[64,24,1792]{2,1,0:T(8,128)(2,1)}, u32[]{:S(2)}, u32[]{:S(2)}) async-start(bf16[64,24,1792]{2,1,0:T(8,128)(2,1)} %bitcast.12), calls=%async_computation.1 | async-start | bytes 11010048 | tf_op jit(solution)/shard_map/all_to_all | solution.py:290
  198.8 0.0 copy-done
  198.8 0.1 copy.7.routes_ref
  198.9 0.0 copy-done.1
  198.9 0.1 copy.8.gates_ref
  198.9 0.5 plan.1
  199.4 4.1 %mix.2.refs_0_ = f32[64,7168]{1,0:T(8,128)S(1)} custom-call(bf16[128,256]{1,0:T(8,128)(2,1)S(1)} %get-tuple-element.8.weights_ref, bf16[1024,1792]{1,0:T(8,128)(2,1)} %bitcast.8.rows_hbm), custom_call_target="tpu_custom_call" | custom-call | flops 939524096 | bytes 3670016 | tf_op jit(solution)/shard_map/mix/pallas_call | solution.py:267
  203.5 61.0 %all-to-all-done.1 = bf16[64,24,1792]{2,1,0:T(8,128)(2,1)} async-done(((bf16[64,24,1792]{2,1,0:T(8,128)(2,1)}), bf16[64,24,1792]{2,1,0:T(8,128)(2,1)}, u32[]{:S(2)}, u32[]{:S(2)}) %all-to-all-start.1) | async-done | bytes 5505056 | tf_op jit(solution)/shard_map/all_to_all | solution.py:290
  264.6 5.1 %mix.3 = bf16[64,7168]{1,0:T(8,128)(2,1)} custom-call(bf16[128,384]{1,0:T(8,128)(2,1)S(1)} %get-tuple-element.7.weights_ref, bf16[1536,1792]{1,0:T(8,128)(2,1)} %bitcast.4.rows_hbm, f32[64,7168]{1,0:T(8,128)S(1)} %mix.2.refs_0_), custom_call_target="tpu_custom_call" | custom-call | flops 1409286144 | bytes 5505024 | tf_op jit(solution)/shard_map/mix/pallas_call | solution.py:267
Async XLA Ops:
  4.0 56.0 %all-to-all-start.2 = ((bf16[64,16,1792]{2,1,0:T(8,128)(2,1)}), bf16[64,16,1792]{2,1,0:T(8,128)(2,1)}, u32[]{:S(2)}, u32[]{:S(2)}) async-start(bf16[64,16,1792]{2,1,0:T(8,128)(2,1)} %bitcast.11), calls=%async_computation.2 | async-start | bytes 7340032 | tf_op jit(solution)/shard_map/all_to_all | solution.py:290
  15.5 53.9 %collective-permute-start = (bf16[1,7168,512]{2,1,0:T(8,128)(2,1)}, bf16[1,7168,512]{2,1,0:T(8,128)(2,1)}, u32[]{:S(2)}, u32[]{:S(2)}) collective-permute-start(bf16[1,7168,512]{2,1,0:T(8,128)(2,1)} %ga.3), channel_id=1, source_target_pairs={{0,1},{1,0},{2,3},{3,2},{4,5},{5,4},{6,7},{7,6},{8,9},{9,8},{10,11... | collective-permute-start | bytes 22020104 | tf_op jit(solution)/shard_map/ppermute | solution.py:296
  15.6 53.9 %collective-permute-start.1 = (bf16[1,7168,512]{2,1,0:T(8,128)(2,1)}, bf16[1,7168,512]{2,1,0:T(8,128)(2,1)}, u32[]{:S(2)}, u32[]{:S(2)}) collective-permute-start(bf16[1,7168,512]{2,1,0:T(8,128)(2,1)} %ua.3), channel_id=1, source_target_pairs={{0,1},{1,0},{2,3},{3,2},{4,5},{5,4},{6,7},{7,6},{8,9},{9,8},{10,11... | collective-permute-start | bytes 22020104 | tf_op jit(solution)/shard_map/ppermute | solution.py:296
  16.1 53.4 %collective-permute-start.2 = (bf16[1,512,7168]{2,1,0:T(8,128)(2,1)}, bf16[1,512,7168]{2,1,0:T(8,128)(2,1)}, u32[]{:S(2)}, u32[]{:S(2)}) collective-permute-start(bf16[1,512,7168]{2,1,0:T(8,128)(2,1)} %da.3), channel_id=1, source_target_pairs={{0,1},{1,0},{2,3},{3,2},{4,5},{5,4},{6,7},{7,6},{8,9},{9,8},{10,11... | collective-permute-start | bytes 22020104 | tf_op jit(solution)/shard_map/ppermute | solution.py:296
  60.0 75.5 %all-to-all-start = ((bf16[64,24,1792]{2,1,0:T(8,128)(2,1)}), bf16[64,24,1792]{2,1,0:T(8,128)(2,1)}, u32[]{:S(2)}, u32[]{:S(2)}) async-start(bf16[64,24,1792]{2,1,0:T(8,128)(2,1)} %bitcast.9), calls=%async_computation | async-start | bytes 11010048 | tf_op jit(solution)/shard_map/all_to_all | solution.py:290
  135.5 54.6 %all-to-all-start.3 = ((bf16[64,16,1792]{2,1,0:T(8,128)(2,1)}), bf16[64,16,1792]{2,1,0:T(8,128)(2,1)}, u32[]{:S(2)}, u32[]{:S(2)}) async-start(bf16[64,16,1792]{2,1,0:T(8,128)(2,1)} %bitcast.10), calls=%async_computation.3 | async-start | bytes 7340032 | tf_op jit(solution)/shard_map/all_to_all | solution.py:290
  190.1 8.7 %copy-start = (s32[64,8]{0,1:T(8,128)S(1)}, s32[64,8]{0,1:T(8,128)}, u32[]{:S(2)}) copy-start(s32[64,8]{0,1:T(8,128)} %param.7) | copy-start | bytes 6148
  190.1 8.8 %copy-start.1 = (f32[64,8]{0,1:T(8,128)S(1)}, f32[64,8]{0,1:T(8,128)}, u32[]{:S(2)}) copy-start(f32[64,8]{0,1:T(8,128)} %param.8) | copy-start | bytes 6148
  190.1 74.5 %all-to-all-start.1 = ((bf16[64,24,1792]{2,1,0:T(8,128)(2,1)}), bf16[64,24,1792]{2,1,0:T(8,128)(2,1)}, u32[]{:S(2)}, u32[]{:S(2)}) async-start(bf16[64,24,1792]{2,1,0:T(8,128)(2,1)} %bitcast.12), calls=%async_computation.1 | async-start | bytes 11010048 | tf_op jit(solution)/shard_map/all_to_all | solution.py:290
